TPU v7x, 32 devices: a whole 2x2x4 slice. The times are simulated.
32 devices in a mesh: az: 16 (over z, y, core), dr: 2 (over x).
Axes of the slice: x: 2, y: 2, z: 4, core: 2. Of those that a mesh axis runs over, the one named last changes fastest.
Arguments:
- stack: bfloat16 [2, 32, 384, 4096], P(None, 'dr', 'az'), may hold values from -6 to 6
- range_filter: float32 [32, 4096], P('dr'), may hold values from 0.2 to 1.5
- scatter_mask: int32 [384, 4096], P('az'), may hold values 0 or 1
Outputs:
- phase_vector: float32 [2, 32, 96, 1024], P(None, None, 'az', 'dr')
All inputs are finite; a program needn't handle non-finite values. No bound on the sum of `scatter_mask` on one device may be relied on, other than what follows from the above.
Results may differ from a plain program's by a relative error of at most 0.0037.
Values may be sent and summed in bfloat16 or wider, within the bound.
A program may use at most 256 MiB of HBM per device.

v0:
```python
import math

import jax
import jax.numpy as jnp
from jax import lax
from jax.sharding import PartitionSpec as P

ITERS = 4


BETA_LOAD = 1.0
PROJ_LOAD = 1.0
SPLIT_MODE = lax.Precision.HIGH
FULL_MODE = lax.Precision.HIGHEST


def padded_2(cells, sides, width):
    for axis, dim in sides:
        count = lax.axis_size(axis)
        ends = count - 1
        head = lax.slice_in_dim(cells, 0, width, axis=dim)
        tail = lax.slice_in_dim(cells, cells.shape[dim] - width, cells.shape[dim], axis=dim)
        cells = jnp.concatenate(
            [
                lax.ppermute(tail, axis, [(i, (i + 1) % count) for i in range(ends)]),
                cells,
                lax.ppermute(head, axis, [((i + 1) % count, i) for i in range(ends)]),
            ],
            axis=dim,
        )
    return cells


def link_phases(cov_real, cov_imag):
    dates = cov_real.shape[0]
    diagonal = cov_real.reshape((dates * dates,) + cov_real.shape[2:])[:: dates + 1]
    scales = jnp.sqrt(diagonal + BETA_LOAD)
    product = scales[:, None] * scales[None, :]
    coh_real = cov_real / product
    coh_imag = cov_imag / product
    vec_real = jnp.ones(diagonal.shape, jnp.float32)
    vec_imag = jnp.zeros(diagonal.shape, jnp.float32)
    for repeat in range(ITERS):
        new_real = jnp.sum(coh_real * vec_real[None] - coh_imag * vec_imag[None], axis=1)
        new_imag = jnp.sum(coh_real * vec_imag[None] + coh_imag * vec_real[None], axis=1)
        length = jnp.sqrt(new_real * new_real + new_imag * new_imag + PROJ_LOAD)
        vec_real = new_real / length
        vec_imag = new_imag / length
    return jnp.stack([vec_real, vec_imag])


def dft_table(count):
    counter = jnp.arange(count, dtype=jnp.int32)
    exponent = counter[:, None] * counter[None, :] % count
    angle = exponent.astype(jnp.float32) * (-2.0 * math.pi / count)
    return (jnp.cos(angle), jnp.sin(angle))


def left_apply(table, values):
    return jnp.einsum("kn,nbc->kbc", table, values, precision=SPLIT_MODE)


def right_apply(values, table):
    return jnp.matmul(values, table, precision=SPLIT_MODE)


def filter_lines(stack, gains):
    dates_here = stack.shape[1]
    lines = stack.shape[2]
    samples = stack.shape[3]
    outer = samples // 128
    batch = dates_here * lines
    first_real, first_imag = dft_table(outer)
    second_real, second_imag = dft_table(128)
    twist_exp = (
        jnp.arange(outer, dtype=jnp.int32)[:, None]
        * jnp.arange(128, dtype=jnp.int32)[None, :]
        % samples
    )
    twist_angle = twist_exp.astype(jnp.float32) * (-2.0 * math.pi / samples)
    twist_real = jnp.cos(twist_angle)[:, None, :]
    twist_imag = jnp.sin(twist_angle)[:, None, :]
    in_real = jnp.transpose(stack[0].reshape(batch, outer, 128), (1, 0, 2)).astype(jnp.float32)
    in_imag = jnp.transpose(stack[1].reshape(batch, outer, 128), (1, 0, 2)).astype(jnp.float32)
    step_real = left_apply(first_real, in_real) - left_apply(first_imag, in_imag)
    step_imag = left_apply(first_real, in_imag) + left_apply(first_imag, in_real)
    turn_real = step_real * twist_real - step_imag * twist_imag
    turn_imag = step_real * twist_imag + step_imag * twist_real
    spec_real = right_apply(turn_real, second_real) - right_apply(turn_imag, second_imag)
    spec_imag = right_apply(turn_real, second_imag) + right_apply(turn_imag, second_real)
    gain_table = jnp.transpose(gains.reshape(dates_here, 128, outer), (2, 0, 1))[:, :, None, :]
    spec_real = (spec_real.reshape(outer, dates_here, lines, 128) * gain_table).reshape(
        outer, batch, 128
    )
    spec_imag = (spec_imag.reshape(outer, dates_here, lines, 128) * gain_table).reshape(
        outer, batch, 128
    )
    back_real = right_apply(spec_real, second_real) + right_apply(spec_imag, second_imag)
    back_imag = right_apply(spec_imag, second_real) - right_apply(spec_real, second_imag)
    untwist_real = back_real * twist_real + back_imag * twist_imag
    untwist_imag = back_imag * twist_real - back_real * twist_imag
    out_real = (
        left_apply(first_real, untwist_real) + left_apply(first_imag, untwist_imag)
    ) / samples
    out_imag = (
        left_apply(first_real, untwist_imag) - left_apply(first_imag, untwist_real)
    ) / samples
    joined = jnp.stack([out_real.astype(jnp.bfloat16), out_imag.astype(jnp.bfloat16)])
    return jnp.transpose(joined, (0, 2, 1, 3)).reshape(2, dates_here, lines, samples)


def on_device(stack, range_filter, scatter_mask):
    parts_dr = lax.axis_size("dr")
    dates = stack.shape[1] * parts_dr
    lines = stack.shape[2]
    samples = stack.shape[3]
    tile = samples // parts_dr
    filtered = filter_lines(stack, range_filter)
    tile_start = lax.axis_index("dr") * tile
    widened = jnp.pad(filtered, ((0, 0), (0, 0), (0, 0), (6, 6)))
    tiles_out = jnp.concatenate(
        [widened[..., number * tile : number * tile + tile + 12] for number in range(parts_dr)],
        axis=3,
    )
    regrouped = lax.all_to_all(tiles_out, "dr", split_axis=3, concat_axis=1, tiled=True)
    mask_wide = jnp.pad(scatter_mask, ((0, 0), (6, 6)))
    mask_tile = lax.dynamic_slice_in_dim(mask_wide, tile_start, tile + 12, 1).astype(jnp.bfloat16)
    joined = jnp.concatenate(
        [regrouped.reshape(2 * dates, lines, tile + 12), mask_tile[None]], axis=0
    )
    padded = padded_2(joined, (("az", 1),), 6)
    width = padded.shape[2]
    weight = padded[2 * dates]
    plain_real = padded[:dates].astype(jnp.float32)
    plain_imag = padded[dates : 2 * dates].astype(jnp.float32)
    masked_real = padded[:dates] * weight[None]
    masked_imag = padded[dates : 2 * dates] * weight[None]
    win_rows = lines // 4
    win_cols = tile // 4
    column = jnp.arange(width, dtype=jnp.int32)[:, None]
    window = jnp.arange(win_cols, dtype=jnp.int32)[None, :]
    band = ((column >= 4 * window) & (column < 4 * window + 16)).astype(jnp.float32)
    group_count = 8
    group_size = dates // group_count

    def one_group(group):
        start = group * group_size
        left_real = lax.dynamic_slice_in_dim(masked_real, start, group_size, 0).astype(jnp.float32)[
            :, None
        ]
        left_imag = lax.dynamic_slice_in_dim(masked_imag, start, group_size, 0).astype(jnp.float32)[
            :, None
        ]
        prod_real = left_real * plain_real[None] + left_imag * plain_imag[None]
        prod_imag = left_imag * plain_real[None] - left_real * plain_imag[None]
        both = jnp.stack([prod_real, prod_imag])
        block_rows = both.reshape(2, group_size, dates, win_rows + 3, 4, width).sum(axis=4)
        row_sum = (
            block_rows[:, :, :, 0:win_rows]
            + block_rows[:, :, :, 1 : win_rows + 1]
            + block_rows[:, :, :, 2 : win_rows + 2]
            + block_rows[:, :, :, 3 : win_rows + 3]
        )
        window_sum = jnp.matmul(row_sum, band, precision=FULL_MODE)
        return (window_sum[0], window_sum[1])

    cov_real, cov_imag = lax.map(one_group, jnp.arange(group_count, dtype=jnp.int32))
    cov_real = cov_real.reshape(dates, dates, win_rows, win_cols)
    cov_imag = cov_imag.reshape(dates, dates, win_rows, win_cols)
    return link_phases(cov_real, cov_imag)


def solution(mesh):
    in_specs = (P(None, "dr", "az", None), P("dr", None), P("az", None))
    out_specs = P(None, None, "az", "dr")
    return jax.shard_map(
        on_device, mesh=mesh, in_specs=in_specs, out_specs=out_specs, check_vma=False
    )
```

profile of v0, /device:TPU:1, one launch (start us, length us, event | category | flops | bytes accessed | tf_op | source)
XLA Modules:
  0.0 1356.1 jit_solution(15803713036484494579)
XLA Ops:
  6.0 4.4 fusion.34
  11.3 4.5 fusion.30
  15.9 8.5 multiply_subtract_fusion.2
  24.4 7.8 fusion.18
  32.2 7.9 fusion.20
  40.8 8.7 bitcast_multiply_fusion.1
  49.6 8.0 fusion.14
  57.6 7.5 fusion.16
  65.1 6.5 bitcast_multiply_fusion
  71.6 7.5 fusion.12
  79.1 14.1 %multiply_add_fusion.1 = (f32[32,384,128]{2,0,1:T(8,128)S(1)}, f32[32,384,128]{2,0,1:T(8,128)}) fusion(f32[32,128]{1,0:T(8,128)S(1)} %get-tuple-element.175, f32[32,128]{1,0:T(8,128)S(1)} %get-tuple-element.176, f32[32,384,128]{2,0,1:T(8,128)} %fusion.14, f32[32,384,128]{2,0,1:T(8,128)} %fusion.16, f32[32,384,128]{2,0,1:T(8,128)} %fusion.12, ...), kind=kOutput, calls=%fused_computation.38 | convolution fusion | flops 1220771840 | bytes 37781504 | tf_op jit(solution)/shard_map/dot_general | solution.py:64
  110.5 10.4 reshape.274
  120.9 5.1 pad_slice_fusion.1
  126.0 4.5 pad_maximum_fusion.1
  130.5 30.8 %copy.160 = bf16[2,16,24,4120]{2,1,0,3:T(8,128)(2,1)} copy(bf16[2,16,24,4120]{3,2,1,0:T(8,128)(2,1)} %pad_maximum_fusion.1) | data formatting | bytes 12656640 | tf_op jit(solution)/shard_map/concatenate | solution.py:121
  161.3 67.7 %reshape.285 = bf16[2,2,791040]{2,1,0:T(2,128)(2,1)} reshape(bf16[4120,2,16,24]{3,2,1,0:T(8,128)(2,1)} %bitcast.130) | data formatting | bytes 12656640
  229.1 6.4 all-to-all-start
  235.7 70.4 %all-to-all-done = bf16[2,2,791040]{2,1,0:T(2,128)(2,1)} async-done(((bf16[2,2,791040]{2,1,0:T(2,128)(2,1)}), bf16[2,2,791040]{2,1,0:T(2,128)(2,1)}, u32[]{:S(2)}, u32[]{:S(2)}) %all-to-all-start) | async-done | bytes 6328352 | tf_op jit(solution)/shard_map/all_to_all | solution.py:125
  306.0 67.1 %reshape.286 = bf16[4120,2,16,24]{3,2,1,0:T(8,128)(2,1)} reshape(bf16[2,2,791040]{2,1,0:T(2,128)(2,1)} %all-to-all-done) | data formatting | bytes 12656640
  373.2 34.9 %copy.161 = bf16[2,16,24,2,2060]{4,2,1,3,0:T(8,128)(2,1)} copy(bf16[2,16,24,2,2060]{2,1,0,4,3:T(8,128)(2,1)} %bitcast.131) | data formatting | bytes 12656640 | tf_op jit(solution)/shard_map/all_to_all | solution.py:125
  412.4 4.7 collective-permute-start
  420.5 37.7 %collective-permute-done = bf16[65,6,2060]{2,0,1:T(8,128)(2,1)} collective-permute-done((bf16[65,6,2060]{2,0,1:T(8,128)(2,1)}, bf16[65,6,2060]{2,0,1:T(8,128)(2,1)}, u32[]{:S(2)}, u32[]{:S(2)}) %collective-permute-start) | collective-permute-done | bytes 1606832 | tf_op jit(solution)/shard_map/ppermute | solution.py:25
  461.8 9.6 pad_maximum_fusion
  471.3 6.5 fusion.172
  477.9 9.9 copy.169
  490.6 6.1 slice_convert_fusion
  496.7 5.6 copy.167
  502.3 5.4 copy.166
  507.7 6.2 broadcast.230
  513.9 6.1 broadcast.230.clone
  520.0 772.4 %while.13 = (s32[]{:T(128)}, f32[8,4,32,6,512]{4,2,3,1,0:T(8,128)}, f32[8,4,32,6,512]{4,2,3,1,0:T(8,128)}, s32[8]{0:T(128)S(1)}, bf16[32,36,2060]{2,0,1:T(8,128)...) while((s32[]{:T(128)}, f32[8,4,32,6,512]{4,2,3,1,0:T(8,128)}, ...), condition=%wide.region_2.3_spmd.clone, body=%wide.region_0.2_spmd.clone.sunk | while | flops 19544489984 | bytes 261074880 | solution.py:167
  524.2 32.1 %multiply_add_fusion.4 = (f32[1,4,32,9,4,2060]{5,2,4,3,1,0:T(8,128)}, f32[1,4,32,9,4,2060]{5,2,4,3,1,0:T(8,128)}) fusion(f32[32,9,4,2060]{3,0,2,1:T(8,128)} %bitcast.122, f32[4,9,4,2060]{3,2,1,0:T(4,128)S(1)} %copy.246, f32[32,9,4,2060]{3,0,2,1:T(8,128)} %bitcast.123, f32[4,9,4,2060]{3,2,1,0:T(4,128)S(1)} %copy.247), kind=kLoop, calls=%fused_computation.3.clone.1 | loop fusion | flops 56954880 | bytes 97297920 | tf_op jit(solution)/shard_map/while/body/eval_jaxpr/add | solution.py:154
  556.4 28.2 %maximum_reduce_fusion.2 = f32[2,4,32,9,2060]{4,2,3,1,0:T(8,128)S(1)} fusion(f32[1,4,32,9,4,2060]{5,2,4,3,1,0:T(8,128)} %get-tuple-element.248, f32[1,4,32,9,4,2060]{5,2,4,3,1,0:T(8,128)} %get-tuple-element.249), kind=kLoop, calls=%fused_computation.1.clone.1 | loop fusion | flops 33223680 | bytes 94924800 | tf_op jit(solution)/shard_map/while/body/eval_jaxpr/reduce_sum | solution.py:157
  584.6 28.1 %fusion.181 = f32[2,4,32,6,512]{4,2,3,1,0:T(8,128)} fusion(f32[2,4,32,9,2060]{4,2,3,1,0:T(8,128)S(1)} %maximum_reduce_fusion.2, s32[512]{0:T(512)S(1)} %get-tuple-element.289, s32[512]{0:T(512)S(1)} %get-tuple-element.288), kind=kOutput, calls=%fused_computation.5.clone.1 | convolution fusion | flops 19454310400 | bytes 56627200 | tf_op jit(solution)/shard_map/while/body/eval_jaxpr/dot_general | solution.py:164
  620.7 32.1 %multiply_add_fusion.4 = (f32[1,4,32,9,4,2060]{5,2,4,3,1,0:T(8,128)}, f32[1,4,32,9,4,2060]{5,2,4,3,1,0:T(8,128)}) fusion(f32[32,9,4,2060]{3,0,2,1:T(8,128)} %bitcast.122, f32[4,9,4,2060]{3,2,1,0:T(4,128)S(1)} %copy.246, f32[32,9,4,2060]{3,0,2,1:T(8,128)} %bitcast.123, f32[4,9,4,2060]{3,2,1,0:T(4,128)S(1)} %copy.247), kind=kLoop, calls=%fused_computation.3.clone.1 | loop fusion | flops 56954880 | bytes 97297920 | tf_op jit(solution)/shard_map/while/body/eval_jaxpr/add | solution.py:154
  652.8 28.2 %maximum_reduce_fusion.2 = f32[2,4,32,9,2060]{4,2,3,1,0:T(8,128)S(1)} fusion(f32[1,4,32,9,4,2060]{5,2,4,3,1,0:T(8,128)} %get-tuple-element.248, f32[1,4,32,9,4,2060]{5,2,4,3,1,0:T(8,128)} %get-tuple-element.249), kind=kLoop, calls=%fused_computation.1.clone.1 | loop fusion | flops 33223680 | bytes 94924800 | tf_op jit(solution)/shard_map/while/body/eval_jaxpr/reduce_sum | solution.py:157
  681.0 28.1 %fusion.181 = f32[2,4,32,6,512]{4,2,3,1,0:T(8,128)} fusion(f32[2,4,32,9,2060]{4,2,3,1,0:T(8,128)S(1)} %maximum_reduce_fusion.2, s32[512]{0:T(512)S(1)} %get-tuple-element.289, s32[512]{0:T(512)S(1)} %get-tuple-element.288), kind=kOutput, calls=%fused_computation.5.clone.1 | convolution fusion | flops 19454310400 | bytes 56627200 | tf_op jit(solution)/shard_map/while/body/eval_jaxpr/dot_general | solution.py:164
  717.1 32.1 %multiply_add_fusion.4 = (f32[1,4,32,9,4,2060]{5,2,4,3,1,0:T(8,128)}, f32[1,4,32,9,4,2060]{5,2,4,3,1,0:T(8,128)}) fusion(f32[32,9,4,2060]{3,0,2,1:T(8,128)} %bitcast.122, f32[4,9,4,2060]{3,2,1,0:T(4,128)S(1)} %copy.246, f32[32,9,4,2060]{3,0,2,1:T(8,128)} %bitcast.123, f32[4,9,4,2060]{3,2,1,0:T(4,128)S(1)} %copy.247), kind=kLoop, calls=%fused_computation.3.clone.1 | loop fusion | flops 56954880 | bytes 97297920 | tf_op jit(solution)/shard_map/while/body/eval_jaxpr/add | solution.py:154
  749.3 28.2 %maximum_reduce_fusion.2 = f32[2,4,32,9,2060]{4,2,3,1,0:T(8,128)S(1)} fusion(f32[1,4,32,9,4,2060]{5,2,4,3,1,0:T(8,128)} %get-tuple-element.248, f32[1,4,32,9,4,2060]{5,2,4,3,1,0:T(8,128)} %get-tuple-element.249), kind=kLoop, calls=%fused_computation.1.clone.1 | loop fusion | flops 33223680 | bytes 94924800 | tf_op jit(solution)/shard_map/while/body/eval_jaxpr/reduce_sum | solution.py:157
  777.5 28.1 %fusion.181 = f32[2,4,32,6,512]{4,2,3,1,0:T(8,128)} fusion(f32[2,4,32,9,2060]{4,2,3,1,0:T(8,128)S(1)} %maximum_reduce_fusion.2, s32[512]{0:T(512)S(1)} %get-tuple-element.289, s32[512]{0:T(512)S(1)} %get-tuple-element.288), kind=kOutput, calls=%fused_computation.5.clone.1 | convolution fusion | flops 19454310400 | bytes 56627200 | tf_op jit(solution)/shard_map/while/body/eval_jaxpr/dot_general | solution.py:164
  805.6 4.2 slice_dynamic-update-slice_fusion.3
  813.8 32.1 %multiply_add_fusion.4 = (f32[1,4,32,9,4,2060]{5,2,4,3,1,0:T(8,128)}, f32[1,4,32,9,4,2060]{5,2,4,3,1,0:T(8,128)}) fusion(f32[32,9,4,2060]{3,0,2,1:T(8,128)} %bitcast.122, f32[4,9,4,2060]{3,2,1,0:T(4,128)S(1)} %copy.246, f32[32,9,4,2060]{3,0,2,1:T(8,128)} %bitcast.123, f32[4,9,4,2060]{3,2,1,0:T(4,128)S(1)} %copy.247), kind=kLoop, calls=%fused_computation.3.clone.1 | loop fusion | flops 56954880 | bytes 97297920 | tf_op jit(solution)/shard_map/while/body/eval_jaxpr/add | solution.py:154
  845.9 28.2 %maximum_reduce_fusion.2 = f32[2,4,32,9,2060]{4,2,3,1,0:T(8,128)S(1)} fusion(f32[1,4,32,9,4,2060]{5,2,4,3,1,0:T(8,128)} %get-tuple-element.248, f32[1,4,32,9,4,2060]{5,2,4,3,1,0:T(8,128)} %get-tuple-element.249), kind=kLoop, calls=%fused_computation.1.clone.1 | loop fusion | flops 33223680 | bytes 94924800 | tf_op jit(solution)/shard_map/while/body/eval_jaxpr/reduce_sum | solution.py:157
  874.1 28.1 %fusion.181 = f32[2,4,32,6,512]{4,2,3,1,0:T(8,128)} fusion(f32[2,4,32,9,2060]{4,2,3,1,0:T(8,128)S(1)} %maximum_reduce_fusion.2, s32[512]{0:T(512)S(1)} %get-tuple-element.289, s32[512]{0:T(512)S(1)} %get-tuple-element.288), kind=kOutput, calls=%fused_computation.5.clone.1 | convolution fusion | flops 19454310400 | bytes 56627200 | tf_op jit(solution)/shard_map/while/body/eval_jaxpr/dot_general | solution.py:164
  902.2 4.1 slice_dynamic-update-slice_fusion.3
  910.3 32.1 %multiply_add_fusion.4 = (f32[1,4,32,9,4,2060]{5,2,4,3,1,0:T(8,128)}, f32[1,4,32,9,4,2060]{5,2,4,3,1,0:T(8,128)}) fusion(f32[32,9,4,2060]{3,0,2,1:T(8,128)} %bitcast.122, f32[4,9,4,2060]{3,2,1,0:T(4,128)S(1)} %copy.246, f32[32,9,4,2060]{3,0,2,1:T(8,128)} %bitcast.123, f32[4,9,4,2060]{3,2,1,0:T(4,128)S(1)} %copy.247), kind=kLoop, calls=%fused_computation.3.clone.1 | loop fusion | flops 56954880 | bytes 97297920 | tf_op jit(solution)/shard_map/while/body/eval_jaxpr/add | solution.py:154
  942.5 28.2 %maximum_reduce_fusion.2 = f32[2,4,32,9,2060]{4,2,3,1,0:T(8,128)S(1)} fusion(f32[1,4,32,9,4,2060]{5,2,4,3,1,0:T(8,128)} %get-tuple-element.248, f32[1,4,32,9,4,2060]{5,2,4,3,1,0:T(8,128)} %get-tuple-element.249), kind=kLoop, calls=%fused_computation.1.clone.1 | loop fusion | flops 33223680 | bytes 94924800 | tf_op jit(solution)/shard_map/while/body/eval_jaxpr/reduce_sum | solution.py:157
  970.7 28.1 %fusion.181 = f32[2,4,32,6,512]{4,2,3,1,0:T(8,128)} fusion(f32[2,4,32,9,2060]{4,2,3,1,0:T(8,128)S(1)} %maximum_reduce_fusion.2, s32[512]{0:T(512)S(1)} %get-tuple-element.289, s32[512]{0:T(512)S(1)} %get-tuple-element.288), kind=kOutput, calls=%fused_computation.5.clone.1 | convolution fusion | flops 19454310400 | bytes 56627200 | tf_op jit(solution)/shard_map/while/body/eval_jaxpr/dot_general | solution.py:164
  1006.9 32.1 %multiply_add_fusion.4 = (f32[1,4,32,9,4,2060]{5,2,4,3,1,0:T(8,128)}, f32[1,4,32,9,4,2060]{5,2,4,3,1,0:T(8,128)}) fusion(f32[32,9,4,2060]{3,0,2,1:T(8,128)} %bitcast.122, f32[4,9,4,2060]{3,2,1,0:T(4,128)S(1)} %copy.246, f32[32,9,4,2060]{3,0,2,1:T(8,128)} %bitcast.123, f32[4,9,4,2060]{3,2,1,0:T(4,128)S(1)} %copy.247), kind=kLoop, calls=%fused_computation.3.clone.1 | loop fusion | flops 56954880 | bytes 97297920 | tf_op jit(solution)/shard_map/while/body/eval_jaxpr/add | solution.py:154
  1039.0 28.2 %maximum_reduce_fusion.2 = f32[2,4,32,9,2060]{4,2,3,1,0:T(8,128)S(1)} fusion(f32[1,4,32,9,4,2060]{5,2,4,3,1,0:T(8,128)} %get-tuple-element.248, f32[1,4,32,9,4,2060]{5,2,4,3,1,0:T(8,128)} %get-tuple-element.249), kind=kLoop, calls=%fused_computation.1.clone.1 | loop fusion | flops 33223680 | bytes 94924800 | tf_op jit(solution)/shard_map/while/body/eval_jaxpr/reduce_sum | solution.py:157
  1067.2 28.1 %fusion.181 = f32[2,4,32,6,512]{4,2,3,1,0:T(8,128)} fusion(f32[2,4,32,9,2060]{4,2,3,1,0:T(8,128)S(1)} %maximum_reduce_fusion.2, s32[512]{0:T(512)S(1)} %get-tuple-element.289, s32[512]{0:T(512)S(1)} %get-tuple-element.288), kind=kOutput, calls=%fused_computation.5.clone.1 | convolution fusion | flops 19454310400 | bytes 56627200 | tf_op jit(solution)/shard_map/while/body/eval_jaxpr/dot_general | solution.py:164
  1103.4 32.1 %multiply_add_fusion.4 = (f32[1,4,32,9,4,2060]{5,2,4,3,1,0:T(8,128)}, f32[1,4,32,9,4,2060]{5,2,4,3,1,0:T(8,128)}) fusion(f32[32,9,4,2060]{3,0,2,1:T(8,128)} %bitcast.122, f32[4,9,4,2060]{3,2,1,0:T(4,128)S(1)} %copy.246, f32[32,9,4,2060]{3,0,2,1:T(8,128)} %bitcast.123, f32[4,9,4,2060]{3,2,1,0:T(4,128)S(1)} %copy.247), kind=kLoop, calls=%fused_computation.3.clone.1 | loop fusion | flops 56954880 | bytes 97297920 | tf_op jit(solution)/shard_map/while/body/eval_jaxpr/add | solution.py:154
  1135.5 28.2 %maximum_reduce_fusion.2 = f32[2,4,32,9,2060]{4,2,3,1,0:T(8,128)S(1)} fusion(f32[1,4,32,9,4,2060]{5,2,4,3,1,0:T(8,128)} %get-tuple-element.248, f32[1,4,32,9,4,2060]{5,2,4,3,1,0:T(8,128)} %get-tuple-element.249), kind=kLoop, calls=%fused_computation.1.clone.1 | loop fusion | flops 33223680 | bytes 94924800 | tf_op jit(solution)/shard_map/while/body/eval_jaxpr/reduce_sum | solution.py:157
  1163.7 28.1 %fusion.181 = f32[2,4,32,6,512]{4,2,3,1,0:T(8,128)} fusion(f32[2,4,32,9,2060]{4,2,3,1,0:T(8,128)S(1)} %maximum_reduce_fusion.2, s32[512]{0:T(512)S(1)} %get-tuple-element.289, s32[512]{0:T(512)S(1)} %get-tuple-element.288), kind=kOutput, calls=%fused_computation.5.clone.1 | convolution fusion | flops 19454310400 | bytes 56627200 | tf_op jit(solution)/shard_map/while/body/eval_jaxpr/dot_general | solution.py:164
  1199.9 32.1 %multiply_add_fusion.4 = (f32[1,4,32,9,4,2060]{5,2,4,3,1,0:T(8,128)}, f32[1,4,32,9,4,2060]{5,2,4,3,1,0:T(8,128)}) fusion(f32[32,9,4,2060]{3,0,2,1:T(8,128)} %bitcast.122, f32[4,9,4,2060]{3,2,1,0:T(4,128)S(1)} %copy.246, f32[32,9,4,2060]{3,0,2,1:T(8,128)} %bitcast.123, f32[4,9,4,2060]{3,2,1,0:T(4,128)S(1)} %copy.247), kind=kLoop, calls=%fused_computation.3.clone.1 | loop fusion | flops 56954880 | bytes 97297920 | tf_op jit(solution)/shard_map/while/body/eval_jaxpr/add | solution.py:154
  1232.0 28.2 %maximum_reduce_fusion.2 = f32[2,4,32,9,2060]{4,2,3,1,0:T(8,128)S(1)} fusion(f32[1,4,32,9,4,2060]{5,2,4,3,1,0:T(8,128)} %get-tuple-element.248, f32[1,4,32,9,4,2060]{5,2,4,3,1,0:T(8,128)} %get-tuple-element.249), kind=kLoop, calls=%fused_computation.1.clone.1 | loop fusion | flops 33223680 | bytes 94924800 | tf_op jit(solution)/shard_map/while/body/eval_jaxpr/reduce_sum | solution.py:157
  1260.2 28.1 %fusion.181 = f32[2,4,32,6,512]{4,2,3,1,0:T(8,128)} fusion(f32[2,4,32,9,2060]{4,2,3,1,0:T(8,128)S(1)} %maximum_reduce_fusion.2, s32[512]{0:T(512)S(1)} %get-tuple-element.289, s32[512]{0:T(512)S(1)} %get-tuple-element.288), kind=kOutput, calls=%fused_computation.5.clone.1 | convolution fusion | flops 19454310400 | bytes 56627200 | tf_op jit(solution)/shard_map/while/body/eval_jaxpr/dot_general | solution.py:164
  1288.3 4.1 slice_dynamic-update-slice_fusion.3
  1292.4 12.1 copy.170
  1304.5 5.3 slice.59
  1310.3 13.3 add_reduce_fusion.3
  1325.8 9.2 add_reduce_fusion.2
  1335.5 9.2 add_reduce_fusion.1
  1345.2 9.4 add_reduce_fusion
  (98 shorter events, 91.5 us)
Async XLA Ops:
  32.2 7.9 copy-start.3
  49.6 15.5 %slice-start.5 = ((s8[6291456]{0:T(1024)(128)(4,1)}), s8[4194304]{0:T(1024)(128)(4,1)S(1)}, s32[]{:S(2)}) async-start(s8[6291456]{0:T(1024)(128)(4,1)} %bitcast.134), calls=%async_computation.6 | async-start | bytes 8388608
  49.6 15.5 %slice-start.7 = ((s8[6291456]{0:T(1024)(128)(4,1)}), s8[4194304]{0:T(1024)(128)(4,1)S(1)}, s32[]{:S(2)}) async-start(s8[6291456]{0:T(1024)(128)(4,1)} %bitcast.140), calls=%async_computation.8 | async-start | bytes 8388608
  57.6 7.5 slice-start.6
  57.6 7.5 slice-start.8
  93.2 3.1 copy-start.1
  229.0 6.5 copy-start.2
  229.1 77.0 %all-to-all-start = ((bf16[2,2,791040]{2,1,0:T(2,128)(2,1)}), bf16[2,2,791040]{2,1,0:T(2,128)(2,1)}, u32[]{:S(2)}, u32[]{:S(2)}) async-start(bf16[2,2,791040]{2,1,0:T(2,128)(2,1)} %reshape.285), calls=%async_computation | async-start | bytes 12656640 | tf_op jit(solution)/shard_map/all_to_all | solution.py:125
  412.4 49.3 %slice-start.3 = ((s8[6684672]{0:T(1024)(128)(4,1)}), s8[2490368]{0:T(1024)(128)(4,1)S(1)}, s32[]{:S(2)}) async-start(s8[6684672]{0:T(1024)(128)(4,1)} %bitcast.125), calls=%async_computation.4 | async-start | bytes 4980736
  412.4 45.8 %collective-permute-start = (bf16[65,6,2060]{2,0,1:T(8,128)(2,1)}, bf16[65,6,2060]{2,0,1:T(8,128)(2,1)}, u32[]{:S(2)}, u32[]{:S(2)}) collective-permute-start(bf16[65,6,2060]{2,0,1:T(8,128)(2,1)} %copy.162), channel_id=1, source_target_pairs={{0,2},{2,4},{4,6},{6,8},{8,10},{10,12},{12,14},{14,16},{16,18},{18... | collective-permute-start | bytes 4820408 | tf_op jit(solution)/shard_map/ppermute | solution.py:25
  418.5 41.4 %collective-permute-start.1 = (bf16[65,6,2060]{2,0,1:T(8,128)(2,1)}, bf16[65,6,2060]{2,0,1:T(8,128)(2,1)}, u32[]{:S(2)}, u32[]{:S(2)}) collective-permute-start(bf16[65,6,2060]{2,0,1:T(8,128)(2,1)} %copy.163), channel_id=1, source_target_pairs={{2,0},{4,2},{6,4},{8,6},{10,8},{12,10},{14,12},{16,14},{18,16},{20... | collective-permute-start | bytes 4820408 | tf_op jit(solution)/shard_map/ppermute | solution.py:27
  420.5 41.3 %slice-start.4 = ((s8[6684672]{0:T(1024)(128)(4,1)}), s8[4194304]{0:T(1024)(128)(4,1)S(1)}, s32[]{:S(2)}) async-start(s8[6684672]{0:T(1024)(128)(4,1)} %bitcast.125), calls=%async_computation.5 | async-start | bytes 8388608
  1310.2 13.8 %slice-start = ((s8[12582912]{0:T(1024)(128)(4,1)}), s8[4194304]{0:T(1024)(128)(4,1)S(1)}, s32[]{:S(2)}) async-start(s8[12582912]{0:T(1024)(128)(4,1)} %bitcast.120), calls=%async_computation.1 | async-start | bytes 8388608
  1310.2 13.8 %slice-start.1 = ((s8[12582912]{0:T(1024)(128)(4,1)}), s8[4194304]{0:T(1024)(128)(4,1)S(1)}, s32[]{:S(2)}) async-start(s8[12582912]{0:T(1024)(128)(4,1)} %bitcast.120), calls=%async_computation.2 | async-start | bytes 8388608
  1310.2 13.8 %slice-start.2 = ((s8[12582912]{0:T(1024)(128)(4,1)}), s8[4194304]{0:T(1024)(128)(4,1)S(1)}, s32[]{:S(2)}) async-start(s8[12582912]{0:T(1024)(128)(4,1)} %bitcast.120), calls=%async_computation.3 | async-start | bytes 8388608
  1310.3 15.5 %copy-start = (f32[8,4,32,6,512]{4,2,3,1,0:T(8,128)S(1)}, f32[8,4,32,6,512]{4,2,3,1,0:T(8,128)}, u32[]{:S(2)}) copy-start(f32[8,4,32,6,512]{4,2,3,1,0:T(8,128)} %get-tuple-element.54) | copy-start | bytes 37748740
where the time goes:
time: 1370 us; the launch traced here: 1360 us
  other arithmetic  560 us (41%)
  local copies, waits for them, and re-layouts  344 us (25%)
  matrix products  326 us (24%)
  waiting for transfers between devices  108 us (8%)
    add x8, other arithmetic, one_group(): prod_real = left_real * plain_real[None] + left_imag * plain_imag[None]  257 us
    reduce_sum x8, other arithmetic, one_group(): both.reshape(2, group_size, dates, win_rows + 3, 4, width).sum(axis=4)  226 us
    dot_general x8, matrix products, one_group(): window_sum = jnp.matmul(row_sum, band, precision=FULL_MODE)  225 us
    unnamed x34, local copies, waits for them, and re-layouts  162 us
    all_to_all x1, waiting for transfers between devices, on_device(): lax.all_to_all(tiles_out, 'dr', split_axis=3, concat_axis=1, tiled=True)  70.4 us
    dot_general x8, matrix products, right_apply(): return jnp.matmul(values, table, precision=SPLIT_MODE)  68.1 us
    reduce_sum x4, other arithmetic, link_phases(): jnp.sum(coh_real * vec_imag[None] + coh_imag * vec_real[None], axis=1)  41.1 us
    ppermute x1, waiting for transfers between devices, padded_2(): lax.ppermute(tail, axis, [(i, (i + 1) % count) for i in range(ends)])  37.7 us
  transfers between devices with their start and end apart: 3, of which 2 were waited for; matrix products, arithmetic and copies ran while one was open for 0% of the time, Pallas kernels for 0%

commit v1 on v0

v1 whole, which is shorter than its diff:
```python
import functools
import math

import jax
import jax.numpy as jnp
import numpy as np
from jax import lax
from jax.experimental import pallas as pl
from jax.experimental.pallas import tpu as pltpu
from jax.sharding import PartitionSpec as P

ITERS = 4
BETA_LOAD = 1.0
PROJ_LOAD = 1.0
LANES = 128
STEP = 256
HALO = 6


def times_const(value, c, s):
    re, im = value
    if abs(s) < 1e-12:
        return (re, im) if c > 0 else (-re, -im)
    if abs(c) < 1e-12:
        return (-im, re) if s > 0 else (im, -re)
    if abs(abs(c) - abs(s)) < 1e-12:
        h = abs(c)
        sc, ss = (1.0 if c > 0 else -1.0), (1.0 if s > 0 else -1.0)
        a = re if sc == 1.0 else -re
        b = im if sc == 1.0 else -im
        return (h * (a - im if ss == 1.0 else a + im), h * (b + re if ss == 1.0 else b - re))
    return (re * c - im * s, re * s + im * c)


def vector_fft(values, sign):
    count = len(values)
    if count == 1:
        return values
    even = vector_fft(values[0::2], sign)
    odd = vector_fft(values[1::2], sign)
    out = [None] * count
    for k in range(count // 2):
        angle = sign * 2.0 * math.pi * k / count
        tr, ti = times_const(odd[k], math.cos(angle), math.sin(angle))
        er, ei = even[k]
        out[k] = (er + tr, ei + ti)
        out[k + count // 2] = (er - tr, ei - ti)
    return out


def filter_kernel(outer, x_ref, gain_ref, twr_ref, twi_ref, fh_ref, fl_ref, bh_ref, bl_ref, out_ref, field, work):
    lines = x_ref.shape[2]
    samples = outer * LANES
    field[...] = x_ref[:, 0].astype(jnp.float32)
    groups = lines // 8

    def forward(g, carry):
        rows = pl.ds(pl.multiple_of(g * 8, 8), 8)
        vals = [
            (field[0, rows, o * LANES : (o + 1) * LANES], field[1, rows, o * LANES : (o + 1) * LANES])
            for o in range(outer)
        ]
        vals = vector_fft(vals, -1.0)
        for o in range(outer):
            re, im = vals[o]
            c, s = twr_ref[o : o + 1, :], twi_ref[o : o + 1, :]
            work[o, rows, 0:LANES] = re * c - im * s
            work[o, rows, LANES:STEP] = re * s + im * c
        return carry

    lax.fori_loop(0, groups, forward, 0)

    def apply(values, high_ref, low_ref):
        high = values.astype(jnp.bfloat16)
        low = (values - high.astype(jnp.float32)).astype(jnp.bfloat16)
        dot = functools.partial(jnp.dot, preferred_element_type=jnp.float32)
        return dot(high, high_ref[...]) + (dot(low, high_ref[...]) + dot(high, low_ref[...]))

    part = 8

    def middle(q, carry):
        span = pl.ds(q * part, part)
        values = work[span].reshape(part * lines, STEP)
        spec = apply(values, fh_ref, fl_ref).reshape(part, lines, STEP)
        gains = gain_ref[0, pl.ds(pl.multiple_of(q * part, part), part), :]
        both = jnp.concatenate([gains, gains], axis=1)[:, None, :]
        spec = (spec * both).reshape(part * lines, STEP)
        work[span] = apply(spec, bh_ref, bl_ref).reshape(part, lines, STEP)
        return carry

    lax.fori_loop(0, outer // part, middle, 0)

    def backward(g, carry):
        rows = pl.ds(pl.multiple_of(g * 8, 8), 8)
        vals = []
        for o in range(outer):
            re, im = work[o, rows, 0:LANES], work[o, rows, LANES:STEP]
            c, s = twr_ref[o : o + 1, :], twi_ref[o : o + 1, :]
            vals.append((re * c + im * s, im * c - re * s))
        vals = vector_fft(vals, 1.0)
        for o in range(outer):
            field[0, rows, o * LANES : (o + 1) * LANES] = vals[o][0] * (1.0 / samples)
            field[1, rows, o * LANES : (o + 1) * LANES] = vals[o][1] * (1.0 / samples)
        return carry

    lax.fori_loop(0, groups, backward, 0)
    out_ref[:, 0] = field[...].astype(jnp.bfloat16)


def split_table(table):
    high = table.astype(jnp.bfloat16)
    return high, (table - np.asarray(high).astype(np.float32)).astype(jnp.bfloat16)


def filter_lines(stack, gains):
    dates, lines, samples = stack.shape[1:]
    outer = samples // LANES
    n = np.arange(LANES)
    angle = -2.0 * np.pi * (n[:, None] * n[None, :] % LANES) / LANES
    c, s = np.cos(angle), np.sin(angle)
    fwd = np.block([[c, s], [-s, c]]).astype(np.float32)
    bwd = np.block([[c, -s], [s, c]]).astype(np.float32)
    twist = -2.0 * np.pi * (np.arange(outer)[:, None] * n[None, :]) / samples
    fh, fl = split_table(fwd)
    bh, bl = split_table(bwd)
    gain_table = jnp.transpose(gains.reshape(dates, LANES, outer), (0, 2, 1))
    whole = lambda *shape: pl.BlockSpec(shape, lambda d: (0,) * len(shape))
    return pl.pallas_call(
        functools.partial(filter_kernel, outer),
        grid=(dates,),
        in_specs=[
            pl.BlockSpec((2, 1, lines, samples), lambda d: (0, d, 0, 0)),
            pl.BlockSpec((1, outer, LANES), lambda d: (d, 0, 0)),
            whole(outer, LANES),
            whole(outer, LANES),
            whole(STEP, STEP),
            whole(STEP, STEP),
            whole(STEP, STEP),
            whole(STEP, STEP),
        ],
        out_specs=pl.BlockSpec((2, 1, lines, samples), lambda d: (0, d, 0, 0)),
        out_shape=jax.ShapeDtypeStruct(stack.shape, jnp.bfloat16),
        scratch_shapes=[
            pltpu.VMEM((2, lines, samples), jnp.float32),
            pltpu.VMEM((outer, lines, STEP), jnp.float32),
        ],
        compiler_params=pltpu.CompilerParams(vmem_limit_bytes=40 * 2**20),
    )(
        stack,
        gain_table,
        np.cos(twist).astype(np.float32),
        np.sin(twist).astype(np.float32),
        fh,
        fl,
        bh,
        bl,
    )


def link_kernel(dates, z_ref, m_ref, band_ref, out_ref, flat, pr, pi, mr, mi, wide, cov_a, cov_b, y_ref, low_ref, diag, m_half):
    step = pl.program_id(0)
    lines = z_ref.shape[1]
    blocks = lines // 4
    wins = blocks - 3
    half = dates // 2
    pitch = flat.shape[1] // (2 * dates)
    rest = wins * 2 * dates

    for p in range(2 * dates):
        rows = z_ref[p].astype(jnp.float32)
        for h in range(2):
            flat[h, p * pitch : p * pitch + lines, :] = rows[:, h * LANES : (h + 1) * LANES]

    for h in range(2):
        m_half[h] = m_ref[:, h * LANES : (h + 1) * LANES]

    def spread(line, carry):
        for h in range(2):
            weight = m_half[h, pl.ds(line, 1), :]
            re = flat[h, pl.ds(line, dates, stride=pitch), :]
            im = flat[h, pl.ds(line + dates * pitch, dates, stride=pitch), :]
            pr[h, line] = re
            pi[h, line] = im
            mr[h, line] = re * weight
            mi[h, line] = im * weight
        return carry

    lax.fori_loop(0, lines, spread, 0)
    odd = step % 2 == 1

    def sums(date, first):
        for h in range(2):
            lanes = slice(h * LANES, (h + 1) * LANES)
            last = None
            pairs = []
            for r in range(blocks):
                re = im = None
                for j in range(4):
                    line = 4 * r + j
                    ar = mr[h, line, pl.ds(date, 1), :]
                    ai = mi[h, line, pl.ds(date, 1), :]
                    br = pr[h, line, first:dates, :]
                    bi = pi[h, line, first:dates, :]
                    t_re = ar * br + ai * bi
                    t_im = ai * br - ar * bi
                    re = t_re if re is None else re + t_re
                    im = t_im if im is None else im + t_im
                if last is not None:
                    pairs.append((last[0] + re, last[1] + im))
                last = (re, im)
                a = r - 3
                if a >= 0:
                    wide[date % 2, a, 0, first:dates, lanes] = (pairs[a][0] + pairs[a + 2][0]).astype(jnp.bfloat16)
                    wide[date % 2, a, 1, first:dates, lanes] = (pairs[a][1] + pairs[a + 2][1]).astype(jnp.bfloat16)

    def gather(date, first):
        rows = wide[date % 2, :, :, first:dates, :].reshape(wins * 2 * (dates - first), STEP)
        total = jnp.dot(rows, band_ref[0], preferred_element_type=jnp.float32)
        total = total.reshape(wins, 2, dates - first, 2 * LANES)
        old = cov_b[date, :, :, first:dates, :]
        cov_a[date, :, :, first:dates, :] = old + total[..., 0:LANES]
        cov_b[date, :, :, first:dates, :] = jnp.where(odd, old, 0.0) + total[..., LANES : 2 * LANES]

    for first, start, stop in ((0, 0, half), (half, half, dates)):
        sums(start, first)

        def body(date, carry, first=first):
            gather(date - 1, first)
            sums(date, first)
            return carry

        lax.fori_loop(start + 1, stop, body, 0)
        gather(stop - 1, first)

    @pl.when((step % 2 == 0) & (step > 0))
    def _():
        def window(a, carry):
            def pick(date, c):
                diag[pl.ds(date, 1), :] = cov_a[date, a, 0, pl.ds(date, 1), :]
                return c

            lax.fori_loop(0, dates, pick, 0)
            inv = 1.0 / jnp.sqrt(diag[...] + BETA_LOAD)
            vec_re = jnp.ones_like(inv)
            vec_im = jnp.zeros_like(inv)
            for repeat in range(ITERS):
                y_ref[0] = vec_re * inv
                y_ref[1] = vec_im * inv
                top_re, top_im = y_ref[0, half:dates], y_ref[1, half:dates]

                def upper(date, acc):
                    acc_re, acc_im = acc
                    c_re, c_im = cov_a[date, a, 0], cov_a[date, a, 1]
                    x_re, x_im = y_ref[0, pl.ds(date, 1), :], y_ref[1, pl.ds(date, 1), :]
                    h_re, h_im = c_re[half:dates], c_im[half:dates]
                    low_ref[0, pl.ds(date, 1), :] = jnp.sum(h_re * top_re - h_im * top_im, axis=0, keepdims=True)
                    low_ref[1, pl.ds(date, 1), :] = jnp.sum(h_re * top_im + h_im * top_re, axis=0, keepdims=True)
                    return (
                        acc_re + (c_re * x_re + c_im * x_im),
                        acc_im + (c_re * x_im - c_im * x_re),
                    )

                def lower(date, acc):
                    acc_re, acc_im = acc
                    c_re, c_im = cov_a[date, a, 0, half:dates], cov_a[date, a, 1, half:dates]
                    x_re, x_im = y_ref[0, pl.ds(date, 1), :], y_ref[1, pl.ds(date, 1), :]
                    return (
                        acc_re + (c_re * x_re + c_im * x_im),
                        acc_im + (c_re * x_im - c_im * x_re),
                    )

                zero = jnp.zeros_like(inv)
                u_re, u_im = lax.fori_loop(0, half, upper, (zero, zero), unroll=4)
                b_re, b_im = lax.fori_loop(half, dates, lower, (u_re[half:], u_im[half:]), unroll=4)
                u_re = jnp.concatenate([u_re[:half] + low_ref[0], b_re], axis=0) * inv
                u_im = jnp.concatenate([u_im[:half] + low_ref[1], b_im], axis=0) * inv
                length = 1.0 / jnp.sqrt(u_re * u_re + u_im * u_im + PROJ_LOAD)
                vec_re = u_re * length
                vec_im = u_im * length
            out_ref[a, 0] = vec_re
            out_ref[a, 1] = vec_im
            return carry

        lax.fori_loop(0, wins, window, 0)


def link_windows(planes, mask, win_cols):
    dates = planes.shape[0] // 2
    lines = planes.shape[1]
    wins = lines // 4 - 3
    chunks = win_cols // LANES
    steps = 2 * chunks + 1
    pitch = -(-lines // 8) * 8
    column = np.arange(STEP)[:, None]
    window = np.arange(LANES)[None, :]
    band = lambda shift: ((column + shift >= 4 * window) & (column + shift < 4 * window + 16)).astype(np.float32)
    zero = np.zeros((STEP, LANES), np.float32)
    bands = np.stack(
        [
            np.concatenate([band(2 * STEP), band(0)], axis=1),
            np.concatenate([zero, band(STEP)], axis=1),
        ]
    ).astype(jnp.bfloat16)
    f32 = jnp.float32
    return pl.pallas_call(
        functools.partial(link_kernel, dates),
        grid=(steps,),
        in_specs=[
            pl.BlockSpec((2 * dates, lines, STEP), lambda t: (0, 0, t)),
            pl.BlockSpec((lines, STEP), lambda t: (0, t)),
            pl.BlockSpec((1, STEP, 2 * LANES), lambda t: (t % 2, 0, 0)),
        ],
        out_specs=pl.BlockSpec((wins, 2, dates, LANES), lambda t: (0, 0, 0, jnp.maximum((t + 1) // 2 - 1, 0))),
        out_shape=jax.ShapeDtypeStruct((wins, 2, dates, win_cols), f32),
        scratch_shapes=[
            pltpu.VMEM((2, 2 * dates * pitch, LANES), f32),
            pltpu.VMEM((2, lines, dates, LANES), f32),
            pltpu.VMEM((2, lines, dates, LANES), f32),
            pltpu.VMEM((2, lines, dates, LANES), f32),
            pltpu.VMEM((2, lines, dates, LANES), f32),
            pltpu.VMEM((2, wins, 2, dates, STEP), jnp.bfloat16),
            pltpu.VMEM((dates, wins, 2, dates, LANES), f32),
            pltpu.VMEM((dates, wins, 2, dates, LANES), f32),
            pltpu.VMEM((2, dates, LANES), f32),
            pltpu.VMEM((2, dates // 2, LANES), f32),
            pltpu.VMEM((dates, LANES), f32),
            pltpu.VMEM((2, lines, LANES), f32),
        ],
        compiler_params=pltpu.CompilerParams(vmem_limit_bytes=56 * 2**20),
    )(planes, mask, bands)


def on_device(stack, range_filter, scatter_mask):
    parts = lax.axis_size("dr")
    own = lax.axis_index("dr")
    dates_here, lines, samples = stack.shape[1:]
    dates = dates_here * parts
    tile = samples // parts
    width = tile + 2 * HALO
    win_cols = tile // 4
    padded_width = STEP * (2 * (win_cols // LANES) + 1)
    filtered = filter_lines(stack, range_filter)
    wide = jnp.pad(filtered, ((0, 0), (0, 0), (0, 0), (HALO, HALO)))

    def cut(array, number):
        return lax.dynamic_slice_in_dim(array, number * tile, width, array.ndim - 1)

    pieces = [cut(wide, own)]
    for shift in range(1, parts):
        sent = cut(wide, lax.rem(own + shift, parts))
        pieces.append(lax.ppermute(sent, "dr", [(i, (i + shift) % parts) for i in range(parts)]))
    planes = jnp.concatenate(pieces, axis=1).reshape(2 * dates, lines, width)
    mask = cut(jnp.pad(scatter_mask, ((0, 0), (HALO, HALO))), own).astype(jnp.bfloat16)

    def halo(array, dim):
        count = lax.axis_size("az")
        head = lax.slice_in_dim(array, 0, HALO, axis=dim)
        tail = lax.slice_in_dim(array, lines - HALO, lines, axis=dim)
        before = lax.ppermute(tail, "az", [(i, i + 1) for i in range(count - 1)])
        after = lax.ppermute(head, "az", [(i + 1, i) for i in range(count - 1)])
        return jnp.concatenate([before, array, after], axis=dim)

    spare = padded_width - width
    planes = jnp.pad(halo(planes, 1), ((0, 0), (0, 0), (0, spare)))
    mask = jnp.pad(halo(mask, 0), ((0, 0), (0, spare))).astype(jnp.float32)
    linked = link_windows(planes, mask, win_cols)
    wins = linked.shape[0]
    linked = jnp.transpose(linked, (1, 2, 0, 3)).reshape(2, parts, dates_here, wins, win_cols)
    ordered = [
        lax.dynamic_index_in_dim(linked, lax.rem(own - t + parts, parts), 1, keepdims=False) for t in range(parts)
    ]
    return jnp.concatenate(ordered, axis=1)


def solution(mesh):
    in_specs = (P(None, "dr", "az", None), P("dr", None), P("az", None))
    out_specs = P(None, None, "az", "dr")
    return jax.shard_map(on_device, mesh=mesh, in_specs=in_specs, out_specs=out_specs, check_vma=False)
```

time: 1370 us -> 356 us (0.26)
  other arithmetic: 560 us -> 15 us
  matrix products: 326 us -> 0 us
  local copies, waits for them, and re-layouts: 344 us -> 25.3 us
  Pallas kernels: 0 us -> 200 us
    dot_general x24 -> x0, matrix products: 326 us -> none  [the longest x8 225 us: one_group(): window_sum = jnp.matmul(row_sum, band, precision=FULL_MODE)]
    reduce_sum x12 -> x0, other arithmetic: 267 us -> none  [the longest x8 226 us: one_group(): both.reshape(2, group_size, dates, win_rows + 3, 4, width).sum(axis=4)]
    add x8 -> x0, other arithmetic: 257 us -> none  [one_group(): prod_real = left_real * plain_real[None] + left_imag * plain_imag[None]]
    pallas_call x0 -> x2, Pallas kernels: none -> 200 us  [the longest x1 153 us: link_windows(): pl.pallas_call(functools.partial(link_kernel, dates), grid=(steps,), in_s...]
    unnamed x34 -> x22, local copies, waits for them, and re-layouts: 162 us -> 9.61 us
    all_to_all x1 -> x0, waiting for transfers between devices: 70.4 us -> none  [on_device(): lax.all_to_all(tiles_out, 'dr', split_axis=3, concat_axis=1, tiled=True)]
    ppermute x2 -> x5, waiting for transfers between devices: 37.7 us -> 99.8 us  [the longest x1 72 us: on_device(): lax.ppermute(sent, 'dr', [(i, (i + shift) % parts) for i in range(parts)])]
    all_to_all x1 -> x0, local copies, waits for them, and re-layouts: 34.9 us -> none  [on_device(): lax.all_to_all(tiles_out, 'dr', split_axis=3, concat_axis=1, tiled=True)]
  transfers between devices with their start and end apart: 3 -> 5, of which waited for: 2 -> 2; matrix products, arithmetic and copies ran while one was open for 0% -> 1% of each run, Pallas kernels for 0% -> 0%
where the time goes in v1:
time: 356 us; the launch traced here: 354 us
  Pallas kernels  200 us (56%)
  waiting for transfers between devices  99.8 us (28%)
  local copies, waits for them, and re-layouts  25.3 us (7%)
  other arithmetic  15 us (4%)
  starting transfers between devices  14.2 us (4%)
    pallas_call x1, Pallas kernels, link_windows(): pl.pallas_call(functools.partial(link_kernel, dates), grid=(steps,), in_s...  153 us
    ppermute x1, waiting for transfers between devices, on_device(): lax.ppermute(sent, 'dr', [(i, (i + shift) % parts) for i in range(parts)])  72 us
    pallas_call x1, Pallas kernels, filter_lines(): pl.pallas_call(functools.partial(filter_kernel, outer), grid=(dates,), in...  47.1 us
    ppermute x2, waiting for transfers between devices, halo(): before = lax.ppermute(tail, 'az', [(i, i + 1) for i in range(count - 1)])  27.7 us
    unnamed x22, local copies, waits for them, and re-layouts  9.61 us
    concatenate x1, other arithmetic, halo(): return jnp.concatenate([before, array, after], axis=dim)  9.47 us
    ppermute x2, starting transfers between devices, halo(): before = lax.ppermute(tail, 'az', [(i, i + 1) for i in range(count - 1)])  8.16 us
  transfers between devices with their start and end apart: 5, of which 2 were waited for; matrix products, arithmetic and copies ran while one was open for 1% of the time, Pallas kernels for 0%

profile of v1, /device:TPU:1, one launch (start us, length us, event | category | flops | bytes accessed | tf_op | source)
XLA Modules:
  0.0 354.3 jit_solution(11438604337167623939)
XLA Ops:
  0.0 1.3 reshape.9
  1.3 0.3 copy.16
  1.6 0.0 copy-start
  1.6 2.8 copy-done
  4.4 0.0 copy-start.1
  4.4 0.9 copy-done.1
  5.3 0.0 copy-start.2
  5.3 0.9 copy-done.2
  6.2 0.0 copy-start.3
  6.2 0.9 copy-done.3
  7.1 0.0 copy-start.4
  7.1 0.9 copy-done.4
  8.0 0.0 copy-start.5
  8.0 0.7 copy-done.5
  8.7 0.0 copy-start.6
  8.7 0.7 copy-done.6
  9.5 47.1 %shard_map.100 = bf16[2,16,24,4096]{3,2,1,0:T(8,128)(2,1)S(1)} custom-call(bf16[2,16,24,4096]{3,2,1,0:T(8,128)(2,1)S(1)} %copy-done, f32[16,32,128]{2,1,0:T(8,128)S(1)} %bitcast.9, f32[32,128]{1,0:T(8,128)S(1)} %copy-done.5, f32[32,128]{1,0:T(8,128)S(1)} %copy-done.6, bf16[256,256]{1,0:T(8,128)(2,1)S(1)} %copy-done.1, bf16[256,256]{1,0:T(8,128)(2,1)S(1)} %copy-done.2, ...), custom_call_target="tpu_custom_call" | custom-call | tf_op jit(solution)/shard_map/pallas_call | solution.py:128
  56.5 5.9 %pad_dynamic-slice_fusion.1 = (bf16[2,16,24,2060]{3,2,1,0:T(8,128)(2,1)}, bf16[2,16,24,2060]{3,2,1,0:T(8,128)(2,1)S(1)}) fusion(s32[]{:T(128)S(6)} %select_n.14, bf16[2,16,24,4096]{3,2,1,0:T(8,128)(2,1)S(1)} %shard_map.100, s32[]{:T(128)S(6)} %select_n.15), kind=kLoop, calls=%fused_computation.8 | loop fusion | bytes 12619784 | tf_op jit(solution)/shard_map/dynamic_slice | solution.py:346
  62.4 2.0 collective-permute-start
  64.4 72.0 %collective-permute-done = bf16[2,16,24,2060]{3,2,1,0:T(8,128)(2,1)S(1)} collective-permute-done((bf16[2,16,24,2060]{3,2,1,0:T(8,128)(2,1)S(1)}, bf16[2,16,24,2060]{3,2,1,0:T(8,128)(2,1)S(1)}, u32[]{:S(2)}, u32[]{:S(2)}) %collective-permute-start) | collective-permute-done | bytes 3164192 | tf_op jit(solution)/shard_map/ppermute | solution.py:351
  136.5 0.0 copy-start.9
  136.5 1.8 copy-done.9
  138.2 3.7 %pad_maximum_fusion = bf16[2,32,24,2060]{3,2,1,0:T(8,128)(2,1)S(1)} fusion(bf16[2,16,24,2060]{3,2,1,0:T(8,128)(2,1)} %copy-done.9, bf16[2,16,24,2060]{3,2,1,0:T(8,128)(2,1)} %get-tuple-element.7), kind=kLoop, calls=%fused_computation.6 | loop fusion | flops 3164160 | bytes 12656640 | tf_op jit(solution)/shard_map/concatenate | solution.py:352
  141.9 0.0 copy-start.7
  141.9 0.0 copy-start.10
  141.9 0.5 fusion.12
  142.5 0.2 copy.17
  142.7 4.5 %collective-permute-start.1 = (bf16[64,6,2060]{2,0,1:T(8,128)(2,1)S(1)}, bf16[64,6,2060]{2,0,1:T(8,128)(2,1)}, u32[]{:S(2)}, u32[]{:S(2)}) collective-permute-start(bf16[64,6,2060]{2,0,1:T(8,128)(2,1)S(1)} %copy.17), channel_id=1, source_target_pairs={{0,2},{2,4},{4,6},{6,8},{8,10},{10,12},{12,14},{14,16},{16,18},{18... | collective-permute-start | bytes 4746248 | tf_op jit(solution)/shard_map/ppermute | solution.py:359
  147.2 1.5 copy.18
  148.7 0.0 copy-done.7
  148.7 1.9 collective-permute-start.2
  150.6 0.0 copy-done.10
  150.6 0.1 fusion.8
  150.8 3.6 %collective-permute-start.3 = (bf16[6,2060]{1,0:T(8,128)(2,1)S(1)}, bf16[6,2060]{1,0:T(8,128)(2,1)S(1)}, u32[]{:S(2)}, u32[]{:S(2)}) collective-permute-start(bf16[6,2060]{1,0:T(8,128)(2,1)S(1)} %get-tuple-element.11), channel_id=1, source_target_pairs={{0,2},{2,4},{4,6},{6,8},{8,10},{10,12},{12,14},{14,16},{16,18},{18... | collective-permute-start | bytes 74168 | tf_op jit(solution)/shard_map/ppermute | solution.py:359
  154.4 2.1 collective-permute-start.4
  156.5 0.0 copy-start.8
  156.5 27.7 %collective-permute-done.3 = bf16[6,2060]{1,0:T(8,128)(2,1)S(1)} collective-permute-done((bf16[6,2060]{1,0:T(8,128)(2,1)S(1)}, bf16[6,2060]{1,0:T(8,128)(2,1)S(1)}, u32[]{:S(2)}, u32[]{:S(2)}) %collective-permute-start.3) | collective-permute-done | bytes 24752 | tf_op jit(solution)/shard_map/ppermute | solution.py:359
  184.3 0.0 collective-permute-done.4
  184.3 0.8 fusion.11.m_ref
  185.1 0.0 collective-permute-done.1
  185.1 2.4 copy.19
  187.5 0.0 collective-permute-done.2
  187.5 2.4 copy.20
  189.9 0.0 copy-done.8
  189.9 9.5 %fusion.4.z_ref = bf16[64,36,2304]{2,1,0:T(8,128)(2,1)} fusion(bf16[64,6,2060]{2,1,0:T(8,128)(2,1)S(1)} %copy.20, bf16[64,24,2060]{2,1,0:T(8,128)(2,1)S(1)} %bitcast.11, bf16[64,6,2060]{2,1,0:T(8,128)(2,1)S(1)} %copy.19), kind=kLoop, calls=%fused_computation.5 | loop fusion | flops 53084160 | bytes 20109312 | tf_op jit(solution)/shard_map/concatenate | solution.py:361
  199.3 152.8 %shard_map.101 = f32[6,2,32,512]{3,2,1,0:T(8,128)} custom-call(bf16[64,36,2304]{2,1,0:T(8,128)(2,1)} %fusion.4.z_ref, f32[36,2304]{1,0:T(8,128)} %fusion.11.m_ref, bf16[2,256,256]{2,1,0:T(8,128)(2,1)} %constant.50.clone.band_ref), custom_call_target="tpu_custom_call" | custom-call | tf_op jit(solution)/shard_map/pallas_call | solution.py:305
  352.2 1.2 constant_dynamic-slice_fusion
  353.3 0.1 copy_bitcast_fusion
  353.4 0.9 pad_maximum_fusion.1
  (1 shorter events, 0.0 us)
Async XLA Ops:
  1.6 2.8 copy-start
  4.4 0.9 copy-start.1
  5.3 0.9 copy-start.2
  6.2 0.9 copy-start.3
  7.1 0.9 copy-start.4
  8.0 0.7 copy-start.5
  8.7 0.7 copy-start.6
  62.4 74.1 %collective-permute-start = (bf16[2,16,24,2060]{3,2,1,0:T(8,128)(2,1)S(1)}, bf16[2,16,24,2060]{3,2,1,0:T(8,128)(2,1)S(1)}, u32[]{:S(2)}, u32[]{:S(2)}) collective-permute-start(bf16[2,16,24,2060]{3,2,1,0:T(8,128)(2,1)S(1)} %get-tuple-element.8), channel_id=1, source_target_pairs={{0,1},{1,0},{2,3},{3,2},{4,5},{5,4},{6,7},{7,6},{8,9},{9,8},{10,11... | collective-permute-start | bytes 9492488 | tf_op jit(solution)/shard_map/ppermute | solution.py:351
  136.5 1.8 copy-start.9
  141.9 6.8 %copy-start.7 = (bf16[2,32,24,2060]{3,2,1,0:T(8,128)(2,1)}, bf16[2,32,24,2060]{3,2,1,0:T(8,128)(2,1)S(1)}, u32[]{:S(2)}) copy-start(bf16[2,32,24,2060]{3,2,1,0:T(8,128)(2,1)S(1)} %pad_maximum_fusion) | copy-start | bytes 18984964
  141.9 8.7 %copy-start.10 = (s32[24,4096]{1,0:T(8,128)S(1)}, s32[24,4096]{1,0:T(8,128)}, u32[]{:S(2)}) copy-start(s32[24,4096]{1,0:T(8,128)} %param.12) | copy-start | bytes 1179652
  142.7 42.4 %collective-permute-start.1 = (bf16[64,6,2060]{2,0,1:T(8,128)(2,1)S(1)}, bf16[64,6,2060]{2,0,1:T(8,128)(2,1)}, u32[]{:S(2)}, u32[]{:S(2)}) collective-permute-start(bf16[64,6,2060]{2,0,1:T(8,128)(2,1)S(1)} %copy.17), channel_id=1, source_target_pairs={{0,2},{2,4},{4,6},{6,8},{8,10},{10,12},{12,14},{14,16},{16,18},{18... | collective-permute-start | bytes 4746248 | tf_op jit(solution)/shard_map/ppermute | solution.py:359
  148.7 38.8 %collective-permute-start.2 = (bf16[64,6,2060]{2,0,1:T(8,128)(2,1)}, bf16[64,6,2060]{2,0,1:T(8,128)(2,1)}, u32[]{:S(2)}, u32[]{:S(2)}) collective-permute-start(bf16[64,6,2060]{2,0,1:T(8,128)(2,1)} %copy.18), channel_id=1, source_target_pairs={{2,0},{4,2},{6,4},{8,6},{10,8},{12,10},{14,12},{16,14},{18,16},{20... | collective-permute-start | bytes 4746248 | tf_op jit(solution)/shard_map/ppermute | solution.py:360
  150.8 33.5 %collective-permute-start.3 = (bf16[6,2060]{1,0:T(8,128)(2,1)S(1)}, bf16[6,2060]{1,0:T(8,128)(2,1)S(1)}, u32[]{:S(2)}, u32[]{:S(2)}) collective-permute-start(bf16[6,2060]{1,0:T(8,128)(2,1)S(1)} %get-tuple-element.11), channel_id=1, source_target_pairs={{0,2},{2,4},{4,6},{6,8},{8,10},{10,12},{12,14},{14,16},{16,18},{18... | collective-permute-start | bytes 74168 | tf_op jit(solution)/shard_map/ppermute | solution.py:359
  154.4 29.9 %collective-permute-start.4 = (bf16[6,2060]{1,0:T(8,128)(2,1)S(1)}, bf16[6,2060]{1,0:T(8,128)(2,1)S(1)}, u32[]{:S(2)}, u32[]{:S(2)}) collective-permute-start(bf16[6,2060]{1,0:T(8,128)(2,1)S(1)} %get-tuple-element.12), channel_id=1, source_target_pairs={{2,0},{4,2},{6,4},{8,6},{10,8},{12,10},{14,12},{16,14},{18,16},{20... | collective-permute-start | bytes 74168 | tf_op jit(solution)/shard_map/ppermute | solution.py:360
  156.5 33.3 %copy-start.8 = (bf16[2,32,24,2060]{3,2,1,0:T(8,128)(2,1)S(1)}, bf16[2,32,24,2060]{3,2,1,0:T(8,128)(2,1)}, u32[]{:S(2)}) copy-start(bf16[2,32,24,2060]{3,2,1,0:T(8,128)(2,1)} %copy-done.7) | copy-start | bytes 18984964

commit v2 on v1

v2 whole, which is shorter than its diff:
```python
import functools
import math

import jax
import jax.numpy as jnp
import numpy as np
from jax import lax
from jax.experimental import pallas as pl
from jax.experimental.pallas import tpu as pltpu
from jax.sharding import PartitionSpec as P

ITERS = 4
BETA_LOAD = 1.0
PROJ_LOAD = 1.0
LANES = 128
STEP = 256
HALO = 6
CHUNKS = 2


def times_const(value, c, s):
    re, im = value
    if abs(s) < 1e-12:
        return (re, im) if c > 0 else (-re, -im)
    if abs(c) < 1e-12:
        return (-im, re) if s > 0 else (im, -re)
    if abs(abs(c) - abs(s)) < 1e-12:
        h = abs(c)
        sc, ss = (1.0 if c > 0 else -1.0), (1.0 if s > 0 else -1.0)
        a = re if sc == 1.0 else -re
        b = im if sc == 1.0 else -im
        return (h * (a - im if ss == 1.0 else a + im), h * (b + re if ss == 1.0 else b - re))
    return (re * c - im * s, re * s + im * c)


def vector_fft(values, sign):
    count = len(values)
    if count == 1:
        return values
    even = vector_fft(values[0::2], sign)
    odd = vector_fft(values[1::2], sign)
    out = [None] * count
    for k in range(count // 2):
        angle = sign * 2.0 * math.pi * k / count
        tr, ti = times_const(odd[k], math.cos(angle), math.sin(angle))
        er, ei = even[k]
        out[k] = (er + tr, ei + ti)
        out[k + count // 2] = (er - tr, ei - ti)
    return out


def filter_kernel(outer, x_ref, gain_ref, twr_ref, twi_ref, tab_ref, out_ref, field, work):
    lines = x_ref.shape[2]
    samples = outer * LANES
    field[...] = x_ref[:, 0].astype(jnp.float32)
    groups = lines // 8

    def forward(g, carry):
        rows = pl.ds(pl.multiple_of(g * 8, 8), 8)
        vals = [
            (field[0, rows, o * LANES : (o + 1) * LANES], field[1, rows, o * LANES : (o + 1) * LANES])
            for o in range(outer)
        ]
        vals = vector_fft(vals, -1.0)
        for o in range(outer):
            re, im = vals[o]
            c, s = twr_ref[o : o + 1, :], twi_ref[o : o + 1, :]
            work[o, rows, 0:LANES] = re * c - im * s
            work[o, rows, LANES:STEP] = re * s + im * c
        return carry

    lax.fori_loop(0, groups, forward, 0)

    def apply(values, way):
        high = values.astype(jnp.bfloat16)
        low = (values - high.astype(jnp.float32)).astype(jnp.bfloat16)
        dot = functools.partial(jnp.dot, preferred_element_type=jnp.float32)
        return dot(high, tab_ref[way]) + (dot(low, tab_ref[way]) + dot(high, tab_ref[way + 2]))

    part = 8

    def middle(q, carry):
        span = pl.ds(q * part, part)
        values = work[span].reshape(part * lines, STEP)
        spec = apply(values, 0).reshape(part, lines, STEP)
        gains = gain_ref[0, pl.ds(pl.multiple_of(q * part, part), part), :]
        both = jnp.concatenate([gains, gains], axis=1)[:, None, :]
        spec = (spec * both).reshape(part * lines, STEP)
        work[span] = apply(spec, 1).reshape(part, lines, STEP)
        return carry

    lax.fori_loop(0, outer // part, middle, 0)

    def backward(g, carry):
        rows = pl.ds(pl.multiple_of(g * 8, 8), 8)
        vals = []
        for o in range(outer):
            re, im = work[o, rows, 0:LANES], work[o, rows, LANES:STEP]
            c, s = twr_ref[o : o + 1, :], twi_ref[o : o + 1, :]
            vals.append((re * c + im * s, im * c - re * s))
        vals = vector_fft(vals, 1.0)
        for o in range(outer):
            field[0, rows, o * LANES : (o + 1) * LANES] = vals[o][0] * (1.0 / samples)
            field[1, rows, o * LANES : (o + 1) * LANES] = vals[o][1] * (1.0 / samples)
        return carry

    lax.fori_loop(0, groups, backward, 0)
    out_ref[:, 0] = field[...].astype(jnp.bfloat16)


def split_table(table):
    high = table.astype(jnp.bfloat16)
    return high, (table - np.asarray(high).astype(np.float32)).astype(jnp.bfloat16)


def filter_lines(stack, gains, chunk, chunks):
    dates, lines, samples = stack.shape[1:]
    here = dates // chunks
    skip = chunk * here
    outer = samples // LANES
    n = np.arange(LANES)
    angle = -2.0 * np.pi * (n[:, None] * n[None, :] % LANES) / LANES
    c, s = np.cos(angle), np.sin(angle)
    fwd = np.block([[c, s], [-s, c]]).astype(np.float32)
    bwd = np.block([[c, -s], [s, c]]).astype(np.float32)
    twist = -2.0 * np.pi * (np.arange(outer)[:, None] * n[None, :]) / samples
    fh, fl = split_table(fwd)
    bh, bl = split_table(bwd)
    gain_table = jnp.transpose(gains.reshape(dates, LANES, outer), (0, 2, 1))
    whole = lambda *shape: pl.BlockSpec(shape, lambda d: (0,) * len(shape))
    return pl.pallas_call(
        functools.partial(filter_kernel, outer),
        grid=(here,),
        in_specs=[
            pl.BlockSpec((2, 1, lines, samples), lambda d: (0, d + skip, 0, 0)),
            pl.BlockSpec((1, outer, LANES), lambda d: (d + skip, 0, 0)),
            whole(outer, LANES),
            whole(outer, LANES),
            whole(4, STEP, STEP),
        ],
        out_specs=pl.BlockSpec((2, 1, lines, samples), lambda d: (0, d, 0, 0)),
        out_shape=jax.ShapeDtypeStruct((2, here, lines, samples), jnp.bfloat16),
        cost_estimate=pl.CostEstimate(flops=here * 10**8, bytes_accessed=10**6, transcendentals=0),
        scratch_shapes=[
            pltpu.VMEM((2, lines, samples), jnp.float32),
            pltpu.VMEM((outer, lines, STEP), jnp.float32),
        ],
        compiler_params=pltpu.CompilerParams(vmem_limit_bytes=40 * 2**20),
    )(
        stack,
        gain_table,
        np.cos(twist).astype(np.float32),
        np.sin(twist).astype(np.float32),
        np.stack([fh, bh, fl, bl]),
    )


def load_planes(groups, m_ref, flat, pr, pi, mr, mi, m_half):
    count, lines = groups[0].shape[1:3]
    dates = count * len(groups)
    pitch = flat.shape[1] // (2 * dates)
    for part in range(2):
        for k, ref in enumerate(groups):
            for p in range(count):
                rows = ref[part, p].astype(jnp.float32)
                place = (part * dates + k * count + p) * pitch
                for h in range(2):
                    flat[h, place : place + lines, :] = rows[:, h * LANES : (h + 1) * LANES]
    for h in range(2):
        m_half[h] = m_ref[:, h * LANES : (h + 1) * LANES]

    def spread(line, carry):
        for h in range(2):
            weight = m_half[h, pl.ds(line, 1), :]
            re = flat[h, pl.ds(line, dates, stride=pitch), :]
            im = flat[h, pl.ds(line + dates * pitch, dates, stride=pitch), :]
            pr[h, line] = re[dates - count :]
            pi[h, line] = im[dates - count :]
            mr[h, line] = re * weight
            mi[h, line] = im * weight
        return carry

    lax.fori_loop(0, lines, spread, 0)


def window_sums(dates, odd, band_ref, pr, pi, mr, mi, wide, cov_a, cov_b):
    count = pr.shape[2]
    blocks = pr.shape[1] // 4
    wins = blocks - 3

    def sums(slot, spot, date):
        for h in range(2):
            lanes = slice(h * LANES, (h + 1) * LANES)
            last = None
            pairs = []
            for r in range(blocks):
                re = im = None
                for j in range(4):
                    line = 4 * r + j
                    ar = mr[h, line, pl.ds(date, 1), :]
                    ai = mi[h, line, pl.ds(date, 1), :]
                    br = pr[h, line]
                    bi = pi[h, line]
                    t_re = ar * br + ai * bi
                    t_im = ai * br - ar * bi
                    re = t_re if re is None else re + t_re
                    im = t_im if im is None else im + t_im
                if last is not None:
                    pairs.append((last[0] + re, last[1] + im))
                last = (re, im)
                a = r - 3
                if a >= 0:
                    wide[slot, spot, a, 0, :, lanes] = (pairs[a][0] + pairs[a + 2][0]).astype(jnp.bfloat16)
                    wide[slot, spot, a, 1, :, lanes] = (pairs[a][1] + pairs[a + 2][1]).astype(jnp.bfloat16)

    def gather(duo):
        rows = wide[duo % 2].reshape(2 * wins * 2 * count, STEP)
        total = jnp.dot(rows, band_ref[0], preferred_element_type=jnp.float32)
        total = total.reshape(2, wins, 2, count, 2 * LANES)
        span = pl.ds(2 * duo, 2)
        old = cov_b[span]
        cov_a[span] = old + total[..., 0:LANES]
        cov_b[span] = jnp.where(odd, old, 0.0) + total[..., LANES : 2 * LANES]

    def both(duo):
        for spot in range(2):
            sums(duo % 2, spot, 2 * duo + spot)

    both(0)

    def body(duo, carry):
        gather(duo - 1)
        both(duo)
        return carry

    lax.fori_loop(1, dates // 2, body, 0)
    gather(dates // 2 - 1)


def own_kernel(z_ref, m_ref, band_ref, cov_ref, flat, pr, pi, mr, mi, m_half, wide, cov_b):
    load_planes([z_ref], m_ref, flat, pr, pi, mr, mi, m_half)
    odd = pl.program_id(0) % 2 == 1
    window_sums(z_ref.shape[1], odd, band_ref, pr, pi, mr, mi, wide, cov_ref, cov_b)


def link_kernel(
    z_ref, z2_ref, m_ref, band_ref, own_ref, out_ref, flat, pr, pi, mr, mi, m_half, wide, cov_b, cov_a, y_ref, low_ref, diag
):
    step = pl.program_id(0)
    half, lines = z_ref.shape[1:3]
    dates = 2 * half
    wins = lines // 4 - 3
    load_planes([z_ref, z2_ref], m_ref, flat, pr, pi, mr, mi, m_half)
    window_sums(dates, step % 2 == 1, band_ref, pr, pi, mr, mi, wide, cov_a, cov_b)

    @pl.when((step % 2 == 0) & (step > 0))
    def _():
        def window(a, carry):
            def pick(date, c):
                diag[pl.ds(date, 1), :] = own_ref[date, a, 0, pl.ds(date, 1), :]
                diag[pl.ds(date + half, 1), :] = cov_a[date + half, a, 0, pl.ds(date, 1), :]
                return c

            lax.fori_loop(0, half, pick, 0)
            inv = 1.0 / jnp.sqrt(diag[...] + BETA_LOAD)
            vec_re = jnp.ones_like(inv)
            vec_im = jnp.zeros_like(inv)

            def add(acc, c_re, c_im, x_re, x_im):
                return (acc[0] + (c_re * x_re + c_im * x_im), acc[1] + (c_re * x_im - c_im * x_re))

            for repeat in range(ITERS):
                y_ref[0] = vec_re * inv
                y_ref[1] = vec_im * inv
                far_re, far_im = y_ref[0, half:dates], y_ref[1, half:dates]

                def turn(date, acc):
                    near, far = acc
                    x_re, x_im = y_ref[0, pl.ds(date, 1), :], y_ref[1, pl.ds(date, 1), :]
                    w_re, w_im = y_ref[0, pl.ds(date + half, 1), :], y_ref[1, pl.ds(date + half, 1), :]
                    h_re, h_im = cov_a[date, a, 0], cov_a[date, a, 1]
                    low_ref[0, pl.ds(date, 1), :] = jnp.sum(h_re * far_re - h_im * far_im, axis=0, keepdims=True)
                    low_ref[1, pl.ds(date, 1), :] = jnp.sum(h_re * far_im + h_im * far_re, axis=0, keepdims=True)
                    near = add(near, own_ref[date, a, 0], own_ref[date, a, 1], x_re, x_im)
                    far = add(far, h_re, h_im, x_re, x_im)
                    far = add(far, cov_a[date + half, a, 0], cov_a[date + half, a, 1], w_re, w_im)
                    return near, far

                zero = jnp.zeros((half, LANES), jnp.float32)
                near, far = lax.fori_loop(0, half, turn, ((zero, zero), (zero, zero)), unroll=8)
                u_re = jnp.concatenate([near[0] + low_ref[0], far[0]], axis=0) * inv
                u_im = jnp.concatenate([near[1] + low_ref[1], far[1]], axis=0) * inv
                length = 1.0 / jnp.sqrt(u_re * u_re + u_im * u_im + PROJ_LOAD)
                vec_re = u_re * length
                vec_im = u_im * length
            out_ref[a, 0] = vec_re
            out_ref[a, 1] = vec_im
            return carry

        lax.fori_loop(0, wins, window, 0)


def call_windows(groups, mask, win_cols, own=None):
    count, lines = groups[0].shape[1:3]
    dates = count * len(groups)
    wins = lines // 4 - 3
    steps = 2 * (win_cols // LANES) + 1
    pitch = -(-lines // 8) * 8
    column = np.arange(STEP)[:, None]
    window = np.arange(LANES)[None, :]
    band = lambda shift: ((column + shift >= 4 * window) & (column + shift < 4 * window + 16)).astype(np.float32)
    zero = np.zeros((STEP, LANES), np.float32)
    bands = np.stack(
        [
            np.concatenate([band(2 * STEP), band(0)], axis=1),
            np.concatenate([zero, band(STEP)], axis=1),
        ]
    ).astype(jnp.bfloat16)
    f32 = jnp.float32
    place = lambda t: jnp.maximum((t + 1) // 2 - 1, 0)
    cov_spec = pl.BlockSpec((count, wins, 2, count, LANES), lambda t: (0, 0, 0, 0, place(t)))
    in_specs = [pl.BlockSpec((2, count, lines, STEP), lambda t: (0, 0, 0, t)) for _ in groups]
    in_specs.append(pl.BlockSpec((lines, STEP), lambda t: (0, t)))
    in_specs.append(pl.BlockSpec((1, STEP, 2 * LANES), lambda t: (t % 2, 0, 0)))
    operands = list(groups) + [mask, bands]
    scratch = [
        pltpu.VMEM((2, 2 * dates * pitch, LANES), f32),
        pltpu.VMEM((2, lines, count, LANES), f32),
        pltpu.VMEM((2, lines, count, LANES), f32),
        pltpu.VMEM((2, lines, dates, LANES), f32),
        pltpu.VMEM((2, lines, dates, LANES), f32),
        pltpu.VMEM((2, lines, LANES), f32),
        pltpu.VMEM((2, 2, wins, 2, count, STEP), jnp.bfloat16),
        pltpu.VMEM((dates, wins, 2, count, LANES), f32),
    ]
    if own is None:
        kernel = own_kernel
        out_spec = cov_spec
        out_shape = (count, wins, 2, count, win_cols)
    else:
        kernel = link_kernel
        in_specs.append(cov_spec)
        operands.append(own)
        out_spec = pl.BlockSpec((wins, 2, dates, LANES), lambda t: (0, 0, 0, place(t)))
        out_shape = (wins, 2, dates, win_cols)
        scratch += [
            pltpu.VMEM((dates, wins, 2, count, LANES), f32),
            pltpu.VMEM((2, dates, LANES), f32),
            pltpu.VMEM((2, count, LANES), f32),
            pltpu.VMEM((dates, LANES), f32),
        ]
    return pl.pallas_call(
        kernel,
        grid=(steps,),
        in_specs=in_specs,
        out_specs=out_spec,
        out_shape=jax.ShapeDtypeStruct(out_shape, f32),
        scratch_shapes=scratch,
        cost_estimate=pl.CostEstimate(flops=steps * 10**8, bytes_accessed=10**6, transcendentals=0),
        compiler_params=pltpu.CompilerParams(vmem_limit_bytes=56 * 2**20),
    )(*operands)


def on_device(stack, range_filter, scatter_mask):
    parts = lax.axis_size("dr")
    own = lax.axis_index("dr")
    dates_here, lines, samples = stack.shape[1:]
    tile = samples // parts
    width = tile + 2 * HALO
    win_cols = tile // 4
    padded_width = STEP * (2 * (win_cols // LANES) + 1)

    def cut(array, number):
        wide = jnp.pad(array, ((0, 0),) * (array.ndim - 1) + ((HALO, HALO),))
        return lax.dynamic_slice_in_dim(wide, number * tile, width, array.ndim - 1)

    def edges(array):
        dim = array.ndim - 2
        count = lax.axis_size("az")
        head = lax.slice_in_dim(array, 0, HALO, axis=dim)
        tail = lax.slice_in_dim(array, lines - HALO, lines, axis=dim)
        before = lax.ppermute(tail, "az", [(i, i + 1) for i in range(count - 1)])
        after = lax.ppermute(head, "az", [(i + 1, i) for i in range(count - 1)])
        return jnp.concatenate([before, array, after], axis=dim)

    def spare(array):
        return jnp.pad(array, ((0, 0),) * (array.ndim - 1) + ((0, padded_width - width),))

    mask = spare(edges(cut(scatter_mask, own).astype(jnp.bfloat16))).astype(jnp.float32)
    pieces = [[] for _ in range(parts)]
    for chunk in range(CHUNKS):
        filtered = filter_lines(stack, range_filter, chunk, CHUNKS)
        sent = [cut(filtered, lax.rem(own + shift, parts)) for shift in range(1, parts)]
        stack, sent = lax.optimization_barrier((stack, sent))
        pieces[0].append(cut(filtered, own))
        for shift in range(1, parts):
            pieces[shift].append(lax.ppermute(sent[shift - 1], "dr", [(i, (i + shift) % parts) for i in range(parts)]))
    near = sum(pieces[: parts // 2], [])
    far = sum(pieces[parts // 2 :], [])
    near = spare(edges(jnp.concatenate(near, axis=1)))
    own_sums = call_windows([near], mask, win_cols)
    own_sums, far = lax.optimization_barrier((own_sums, far))
    far = spare(edges(jnp.concatenate(far, axis=1)))
    linked = call_windows([near, far], mask, win_cols, own_sums)
    wins = linked.shape[0]
    linked = jnp.transpose(linked, (1, 2, 0, 3)).reshape(2, parts, dates_here, wins, win_cols)
    ordered = [
        lax.dynamic_index_in_dim(linked, lax.rem(own - t + parts, parts), 1, keepdims=False) for t in range(parts)
    ]
    return jnp.concatenate(ordered, axis=1)


def solution(mesh):
    in_specs = (P(None, "dr", "az", None), P("dr", None), P("az", None))
    out_specs = P(None, None, "az", "dr")
    return jax.shard_map(on_device, mesh=mesh, in_specs=in_specs, out_specs=out_specs, check_vma=False)
```

time: 356 us -> 291 us (0.82)
  waiting for transfers between devices: 99.8 us -> 33.8 us
  starting transfers between devices: 14.2 us -> 20.1 us
    ppermute x5 -> x8, waiting for transfers between devices: 99.8 us -> 33.8 us  [the longest x3 19.9 us: edges(): before = lax.ppermute(tail, 'az', [(i, i + 1) for i in range(count - 1)])]
    ppermute x5 -> x8, starting transfers between devices: 14.2 us -> 20.1 us  [the longest x3 11.3 us: edges(): before = lax.ppermute(tail, 'az', [(i, i + 1) for i in range(count - 1)])]
    unnamed x22 -> x13, local copies, waits for them, and re-layouts: 9.61 us -> 8.01 us
    pallas_call x2 -> x4, Pallas kernels: 200 us -> 201 us  [the longest x2 153 us: call_windows(): pl.pallas_call(kernel, grid=(steps,), in_specs=in_specs, out_specs=out_sp...]
  transfers between devices with their start and end apart: 5 -> 8, of which waited for: 2 -> 4; matrix products, arithmetic and copies ran while one was open for 1% -> 3% of each run, Pallas kernels for 0% -> 15%
where the time goes in v2:
time: 291 us; the launch traced here: 290 us
  Pallas kernels  201 us (69%)
  waiting for transfers between devices  33.8 us (12%)
  local copies, waits for them, and re-layouts  22 us (8%)
  starting transfers between devices  20.1 us (7%)
  other arithmetic  13.7 us (5%)
    pallas_call x2, Pallas kernels, call_windows(): pl.pallas_call(kernel, grid=(steps,), in_specs=in_specs, out_specs=out_sp...  153 us
    pallas_call x2, Pallas kernels, filter_lines(): pl.pallas_call(functools.partial(filter_kernel, outer), grid=(here,), in_...  47.2 us
    ppermute x3, waiting for transfers between devices, edges(): before = lax.ppermute(tail, 'az', [(i, i + 1) for i in range(count - 1)])  19.9 us
    concatenate x2, other arithmetic, edges(): return jnp.concatenate([before, array, after], axis=dim)  11.6 us
    ppermute x3, starting transfers between devices, edges(): before = lax.ppermute(tail, 'az', [(i, i + 1) for i in range(count - 1)])  11.3 us
    unnamed x13, local copies, waits for them, and re-layouts  8.01 us
    ppermute x3, waiting for transfers between devices, edges(): after = lax.ppermute(head, 'az', [(i + 1, i) for i in range(count - 1)])  7.38 us
    ppermute x2, waiting for transfers between devices, on_device(): lax.ppermute(sent[shift - 1], 'dr', [(i, (i + shift) % parts) for i in ra...  6.48 us
  transfers between devices with their start and end apart: 8, of which 4 were waited for; matrix products, arithmetic and copies ran while one was open for 3% of the time, Pallas kernels for 15%

profile of v2, /device:TPU:1, one launch (start us, length us, event | category | flops | bytes accessed | tf_op | source)
XLA Modules:
  0.0 290.3 jit_solution(4099651491749515113)
XLA Ops:
  0.0 1.3 reshape.7
  1.3 0.3 copy.17
  1.6 0.0 copy-start
  1.6 2.8 copy-done
  4.4 0.0 copy-start.1
  4.4 1.0 copy-done.1
  5.4 0.0 copy-start.2
  5.4 0.7 copy-done.2
  6.2 0.0 copy-start.3
  6.2 0.7 copy-done.3
  6.9 23.6 %shard_map.109 = bf16[2,8,24,4096]{3,2,1,0:T(8,128)(2,1)S(1)} custom-call(bf16[2,16,24,4096]{3,2,1,0:T(8,128)(2,1)S(1)} %copy-done, f32[16,32,128]{2,1,0:T(8,128)S(1)} %bitcast.8, f32[32,128]{1,0:T(8,128)S(1)} %copy-done.3, f32[32,128]{1,0:T(8,128)S(1)} %copy-done.2, bf16[4,256,256]{2,1,0:T(8,128)(2,1)S(1)} %copy-done.1), custom_call_target="tpu_custom_call" | custom-call | flops 800000000 | bytes 1000000 | tf_op jit(solution)/shard_map/pallas_call | solution.py:131
  30.5 2.0 pad_dynamic-slice_fusion.3
  32.5 23.6 %shard_map.110 = bf16[2,8,24,4096]{3,2,1,0:T(8,128)(2,1)S(1)} custom-call(bf16[2,16,24,4096]{3,2,1,0:T(8,128)(2,1)S(1)} %copy-done, f32[16,32,128]{2,1,0:T(8,128)S(1)} %bitcast.9, f32[32,128]{1,0:T(8,128)S(1)} %copy-done.3, f32[32,128]{1,0:T(8,128)S(1)} %copy-done.2, bf16[4,256,256]{2,1,0:T(8,128)(2,1)S(1)} %copy-done.1), custom_call_target="tpu_custom_call" | custom-call | flops 800000000 | bytes 1000000 | tf_op jit(solution)/shard_map/pallas_call | solution.py:131
  56.1 2.0 pad_dynamic-slice_fusion
  58.1 0.3 pad_maximum_fusion.1
  58.4 0.0 copy-start.5
  58.4 0.1 copy.19
  58.5 2.1 collective-permute-start.1
  60.6 0.1 copy.18
  60.7 4.5 %collective-permute-start = (bf16[2,16,6,2060]{3,1,2,0:T(8,128)(2,1)S(1)}, bf16[2,16,6,2060]{3,1,2,0:T(8,128)(2,1)S(1)}, u32[]{:S(2)}, u32[]{:S(2)}) collective-permute-start(bf16[2,16,6,2060]{3,1,2,0:T(8,128)(2,1)S(1)} %copy.18), channel_id=1, source_target_pairs={{0,2},{2,4},{4,6},{6,8},{8,10},{10,12},{12,14},{14,16},{16,18},{18... | collective-permute-start | bytes 2373128 | tf_op jit(solution)/shard_map/ppermute | solution.py:382
  65.2 0.0 copy-done.5
  65.2 0.1 fusion.15
  65.3 2.4 collective-permute-start.2
  67.8 1.9 collective-permute-start.3
  69.7 1.3 collective-permute-start.4
  71.0 12.2 %collective-permute-done.2 = bf16[6,2060]{1,0:T(8,128)(2,1)S(1)} collective-permute-done((bf16[6,2060]{1,0:T(8,128)(2,1)S(1)}, bf16[6,2060]{1,0:T(8,128)(2,1)S(1)}, u32[]{:S(2)}, u32[]{:S(2)}) %collective-permute-start.2) | collective-permute-done | bytes 24752 | tf_op jit(solution)/shard_map/ppermute | solution.py:382
  83.2 1.2 collective-permute-start.5
  84.4 0.0 collective-permute-done.3
  84.4 0.8 fusion.18.m_ref
  85.2 0.0 collective-permute-done.1
  85.2 0.2 copy.21
  85.4 0.0 collective-permute-done
  85.4 0.2 copy.20
  85.6 6.2 %fusion.8.z_ref = bf16[2,16,36,2304]{3,2,1,0:T(8,128)(2,1)} fusion(bf16[2,16,6,2060]{3,2,1,0:T(8,128)(2,1)S(1)} %copy.21, bf16[2,16,6,2060]{3,2,1,0:T(8,128)(2,1)S(1)} %copy.20, bf16[2,8,24,2060]{3,2,1,0:T(8,128)(2,1)S(1)} %get-tuple-element.22, bf16[2,8,24,2060]{3,2,1,0:T(8,128)(2,1)S(1)} %get-tuple-element.23), kind=kLoop, calls=%fused_computation.9 | loop fusion | flops 34504704 | bytes 10054656 | tf_op jit(solution)/shard_map/concatenate | solution.py:384
  91.8 44.4 %shard_map.111.own_ref = f32[16,6,2,16,512]{4,3,2,1,0:T(8,128)} custom-call(bf16[2,16,36,2304]{3,2,1,0:T(8,128)(2,1)} %fusion.8.z_ref, f32[36,2304]{1,0:T(8,128)} %fusion.18.m_ref, bf16[2,256,256]{2,1,0:T(8,128)(2,1)} %constant.41.clone.band_ref), custom_call_target="tpu_custom_call" | custom-call | flops 900000000 | bytes 1000000 | tf_op jit(solution)/shard_map/pallas_call | solution.py:352
  136.2 0.0 collective-permute-done.4
  136.2 0.0 copy-start.4
  136.2 1.2 copy-done.4
  137.4 6.5 %collective-permute-done.5 = bf16[2,8,24,2060]{3,2,1,0:T(8,128)(2,1)} collective-permute-done((bf16[2,8,24,2060]{3,2,1,0:T(8,128)(2,1)S(1)}, bf16[2,8,24,2060]{3,2,1,0:T(8,128)(2,1)}, u32[]{:S(2)}, u32[]{:S(2)}) %collective-permute-start.5) | collective-permute-done | bytes 1582112 | tf_op jit(solution)/shard_map/ppermute | solution.py:397
  143.9 1.6 constant_dynamic-update-slice_fusion.1
  145.4 1.7 constant_dynamic-update-slice_fusion
  147.1 0.3 fusion.19
  147.4 1.0 copy.23
  148.4 2.3 collective-permute-start.7
  150.7 1.0 copy.22
  151.7 4.4 %collective-permute-start.6 = (bf16[2,16,6,2060]{3,1,2,0:T(8,128)(2,1)}, bf16[2,16,6,2060]{3,1,2,0:T(8,128)(2,1)}, u32[]{:S(2)}, u32[]{:S(2)}) collective-permute-start(bf16[2,16,6,2060]{3,1,2,0:T(8,128)(2,1)} %copy.22), channel_id=1, source_target_pairs={{0,2},{2,4},{4,6},{6,8},{8,10},{10,12},{12,14},{14,16},{16,18},{18... | collective-permute-start | bytes 2373128 | tf_op jit(solution)/shard_map/ppermute | solution.py:382
  156.1 7.4 %collective-permute-done.7 = bf16[2,16,6,2060]{3,1,2,0:T(8,128)(2,1)} collective-permute-done((bf16[2,16,6,2060]{3,1,2,0:T(8,128)(2,1)}, bf16[2,16,6,2060]{3,1,2,0:T(8,128)(2,1)}, u32[]{:S(2)}, u32[]{:S(2)}) %collective-permute-start.7) | collective-permute-done | bytes 791072 | tf_op jit(solution)/shard_map/ppermute | solution.py:383
  163.5 1.3 copy.25
  164.8 7.7 %collective-permute-done.6 = bf16[2,16,6,2060]{3,1,2,0:T(8,128)(2,1)} collective-permute-done((bf16[2,16,6,2060]{3,1,2,0:T(8,128)(2,1)}, bf16[2,16,6,2060]{3,1,2,0:T(8,128)(2,1)}, u32[]{:S(2)}, u32[]{:S(2)}) %collective-permute-start.6) | collective-permute-done | bytes 791072 | tf_op jit(solution)/shard_map/ppermute | solution.py:382
  172.5 1.3 copy.24
  173.8 5.4 %fusion.11.z2_ref = bf16[2,16,36,2304]{3,2,1,0:T(8,128)(2,1)} fusion(bf16[2,16,6,2060]{3,2,1,0:T(8,128)(2,1)S(1)} %copy.25, bf16[2,16,24,2060]{3,2,1,0:T(8,128)(2,1)S(1)} %constant_dynamic-update-slice_fusion, bf16[2,16,6,2060]{3,2,1,0:T(8,128)(2,1)S(1)} %copy.24), kind=kLoop, calls=%fused_computation.12 | loop fusion | flops 26542080 | bytes 10054656 | tf_op jit(solution)/shard_map/concatenate | solution.py:384
  179.2 109.0 %shard_map.112 = f32[6,2,32,512]{3,2,1,0:T(8,128)} custom-call(bf16[2,16,36,2304]{3,2,1,0:T(8,128)(2,1)} %fusion.8.z_ref, bf16[2,16,36,2304]{3,2,1,0:T(8,128)(2,1)} %fusion.11.z2_ref, f32[36,2304]{1,0:T(8,128)} %fusion.18.m_ref, bf16[2,256,256]{2,1,0:T(8,128)(2,1)} %constant.41.clone.band_ref, f32[16,6,2,16,512]{4,3,2,1,0:T(8,128)} %shard_map.111.own_ref), custom_call_target="tpu_custom_call" | custom-call | flops 900000000 | bytes 1000000 | tf_op jit(solution)/shard_map/pallas_call | solution.py:352
  288.2 1.2 constant_dynamic-slice_fusion
  289.3 0.1 copy_bitcast_fusion
  289.4 0.9 pad_maximum_fusion.2
  (1 shorter events, 0.0 us)
Async XLA Ops:
  1.6 2.8 copy-start
  4.4 1.0 copy-start.1
  5.4 0.7 copy-start.2
  6.2 0.7 copy-start.3
  58.4 6.8 %copy-start.5 = (s32[24,4096]{1,0:T(8,128)S(1)}, s32[24,4096]{1,0:T(8,128)}, u32[]{:S(2)}) copy-start(s32[24,4096]{1,0:T(8,128)} %param.13) | copy-start | bytes 1179652
  58.5 26.7 %collective-permute-start.1 = (bf16[2,16,6,2060]{3,1,2,0:T(8,128)(2,1)S(1)}, bf16[2,16,6,2060]{3,1,2,0:T(8,128)(2,1)S(1)}, u32[]{:S(2)}, u32[]{:S(2)}) collective-permute-start(bf16[2,16,6,2060]{3,1,2,0:T(8,128)(2,1)S(1)} %copy.19), channel_id=1, source_target_pairs={{2,0},{4,2},{6,4},{8,6},{10,8},{12,10},{14,12},{16,14},{18,16},{20... | collective-permute-start | bytes 2373128 | tf_op jit(solution)/shard_map/ppermute | solution.py:383
  60.7 24.7 %collective-permute-start = (bf16[2,16,6,2060]{3,1,2,0:T(8,128)(2,1)S(1)}, bf16[2,16,6,2060]{3,1,2,0:T(8,128)(2,1)S(1)}, u32[]{:S(2)}, u32[]{:S(2)}) collective-permute-start(bf16[2,16,6,2060]{3,1,2,0:T(8,128)(2,1)S(1)} %copy.18), channel_id=1, source_target_pairs={{0,2},{2,4},{4,6},{6,8},{8,10},{10,12},{12,14},{14,16},{16,18},{18... | collective-permute-start | bytes 2373128 | tf_op jit(solution)/shard_map/ppermute | solution.py:382
  65.3 17.9 %collective-permute-start.2 = (bf16[6,2060]{1,0:T(8,128)(2,1)S(1)}, bf16[6,2060]{1,0:T(8,128)(2,1)S(1)}, u32[]{:S(2)}, u32[]{:S(2)}) collective-permute-start(bf16[6,2060]{1,0:T(8,128)(2,1)S(1)} %get-tuple-element.27), channel_id=1, source_target_pairs={{0,2},{2,4},{4,6},{6,8},{8,10},{10,12},{12,14},{14,16},{16,18},{18... | collective-permute-start | bytes 74168 | tf_op jit(solution)/shard_map/ppermute | solution.py:382
  67.8 16.7 %collective-permute-start.3 = (bf16[6,2060]{1,0:T(8,128)(2,1)S(1)}, bf16[6,2060]{1,0:T(8,128)(2,1)S(1)}, u32[]{:S(2)}, u32[]{:S(2)}) collective-permute-start(bf16[6,2060]{1,0:T(8,128)(2,1)S(1)} %get-tuple-element.28), channel_id=1, source_target_pairs={{2,0},{4,2},{6,4},{8,6},{10,8},{12,10},{14,12},{16,14},{18,16},{20... | collective-permute-start | bytes 74168 | tf_op jit(solution)/shard_map/ppermute | solution.py:383
  69.7 66.5 %collective-permute-start.4 = (bf16[2,8,24,2060]{3,2,1,0:T(8,128)(2,1)S(1)}, bf16[2,8,24,2060]{3,2,1,0:T(8,128)(2,1)S(1)}, u32[]{:S(2)}, u32[]{:S(2)}) collective-permute-start(bf16[2,8,24,2060]{3,2,1,0:T(8,128)(2,1)S(1)} %get-tuple-element.12), channel_id=1, source_target_pairs={{0,1},{1,0},{2,3},{3,2},{4,5},{5,4},{6,7},{7,6},{8,9},{9,8},{10,11... | collective-permute-start | bytes 4746248 | tf_op jit(solution)/shard_map/ppermute | solution.py:397
  83.2 60.7 %collective-permute-start.5 = (bf16[2,8,24,2060]{3,2,1,0:T(8,128)(2,1)S(1)}, bf16[2,8,24,2060]{3,2,1,0:T(8,128)(2,1)}, u32[]{:S(2)}, u32[]{:S(2)}) collective-permute-start(bf16[2,8,24,2060]{3,2,1,0:T(8,128)(2,1)S(1)} %get-tuple-element.13), channel_id=1, source_target_pairs={{0,1},{1,0},{2,3},{3,2},{4,5},{5,4},{6,7},{7,6},{8,9},{9,8},{10,11... | collective-permute-start | bytes 4746248 | tf_op jit(solution)/shard_map/ppermute | solution.py:397
  136.2 1.2 copy-start.4
  148.4 15.1 %collective-permute-start.7 = (bf16[2,16,6,2060]{3,1,2,0:T(8,128)(2,1)}, bf16[2,16,6,2060]{3,1,2,0:T(8,128)(2,1)}, u32[]{:S(2)}, u32[]{:S(2)}) collective-permute-start(bf16[2,16,6,2060]{3,1,2,0:T(8,128)(2,1)} %copy.23), channel_id=1, source_target_pairs={{2,0},{4,2},{6,4},{8,6},{10,8},{12,10},{14,12},{16,14},{18,16},{20... | collective-permute-start | bytes 2373128 | tf_op jit(solution)/shard_map/ppermute | solution.py:383
  151.7 20.8 %collective-permute-start.6 = (bf16[2,16,6,2060]{3,1,2,0:T(8,128)(2,1)}, bf16[2,16,6,2060]{3,1,2,0:T(8,128)(2,1)}, u32[]{:S(2)}, u32[]{:S(2)}) collective-permute-start(bf16[2,16,6,2060]{3,1,2,0:T(8,128)(2,1)} %copy.22), channel_id=1, source_target_pairs={{0,2},{2,4},{4,6},{6,8},{8,10},{10,12},{12,14},{14,16},{16,18},{18... | collective-permute-start | bytes 2373128 | tf_op jit(solution)/shard_map/ppermute | solution.py:382

commit v3 on v2

--- a/solution.py
+++ b/solution.py
@@ -15,7 +15,6 @@
 LANES = 128
 STEP = 256
 HALO = 6
-CHUNKS = 2
 
 
 def times_const(value, c, s):
@@ -113,10 +112,8 @@
     return high, (table - np.asarray(high).astype(np.float32)).astype(jnp.bfloat16)
 
 
-def filter_lines(stack, gains, chunk, chunks):
+def filter_lines(stack, gains, skip, here):
     dates, lines, samples = stack.shape[1:]
-    here = dates // chunks
-    skip = chunk * here
     outer = samples // LANES
     n = np.arange(LANES)
     angle = -2.0 * np.pi * (n[:, None] * n[None, :] % LANES) / LANES
@@ -155,17 +152,29 @@
     )
 
 
-def load_planes(groups, m_ref, flat, pr, pi, mr, mi, m_half):
-    count, lines = groups[0].shape[1:3]
+def load_planes(width, groups, m_ref, flat, pr, pi, mr, mi, m_half):
+    count = groups[0][-1].shape[1]
+    lines = m_ref.shape[0]
     dates = count * len(groups)
     pitch = flat.shape[1] // (2 * dates)
+    column = lax.broadcasted_iota(jnp.int32, (1, STEP), 1) + pl.program_id(0) * STEP
+    inside = column < width
+
+    def put(ref, part, p, place):
+        rows = jnp.where(inside, ref[part, p].astype(jnp.float32), 0.0)
+        for h in range(2):
+            flat[h, place : place + rows.shape[0], :] = rows[:, h * LANES : (h + 1) * LANES]
+
     for part in range(2):
-        for k, ref in enumerate(groups):
+        for k, (*middle, before, after) in enumerate(groups):
+            place = (part * dates + k * count) * pitch
             for p in range(count):
-                rows = ref[part, p].astype(jnp.float32)
-                place = (part * dates + k * count + p) * pitch
-                for h in range(2):
-                    flat[h, place : place + lines, :] = rows[:, h * LANES : (h + 1) * LANES]
+                put(before, part, p, place + p * pitch)
+                put(after, part, p, place + p * pitch + lines - HALO)
+            for ref in middle:
+                for p in range(ref.shape[1]):
+                    put(ref, part, p, place + HALO)
+                    place += pitch
     for h in range(2):
         m_half[h] = m_ref[:, h * LANES : (h + 1) * LANES]
 
@@ -183,13 +192,13 @@
     lax.fori_loop(0, lines, spread, 0)
 
 
-def window_sums(dates, odd, band_ref, pr, pi, mr, mi, wide, cov_a, cov_b):
+def window_sums(halves, dates, odd, band_ref, pr, pi, mr, mi, wide, cov_a, cov_b):
     count = pr.shape[2]
     blocks = pr.shape[1] // 4
     wins = blocks - 3
 
     def sums(slot, spot, date):
-        for h in range(2):
+        for h in range(halves):
             lanes = slice(h * LANES, (h + 1) * LANES)
             last = None
             pairs = []
@@ -237,21 +246,32 @@
     gather(dates // 2 - 1)
 
 
-def own_kernel(z_ref, m_ref, band_ref, cov_ref, flat, pr, pi, mr, mi, m_half, wide, cov_b):
-    load_planes([z_ref], m_ref, flat, pr, pi, mr, mi, m_half)
-    odd = pl.program_id(0) % 2 == 1
-    window_sums(z_ref.shape[1], odd, band_ref, pr, pi, mr, mi, wide, cov_ref, cov_b)
-
-
-def link_kernel(
-    z_ref, z2_ref, m_ref, band_ref, own_ref, out_ref, flat, pr, pi, mr, mi, m_half, wide, cov_b, cov_a, y_ref, low_ref, diag
-):
+def all_sums(dates, *refs):
     step = pl.program_id(0)
-    half, lines = z_ref.shape[1:3]
+    last = step == pl.num_programs(0) - 1
+    odd = step % 2 == 1
+    pl.when(last)(lambda: window_sums(1, dates, odd, *refs))
+    pl.when(jnp.logical_not(last))(lambda: window_sums(2, dates, odd, *refs))
+
+
+def own_kernel(width, sizes, *refs):
+    group = refs[: sizes[0]]
+    m_ref, band_ref, cov_ref, flat, pr, pi, mr, mi, m_half, wide, cov_b = refs[sizes[0] :]
+    load_planes(width, [group], m_ref, flat, pr, pi, mr, mi, m_half)
+    all_sums(group[-1].shape[1], band_ref, pr, pi, mr, mi, wide, cov_ref, cov_b)
+
+
+def link_kernel(width, sizes, *refs):
+    groups = [refs[: sizes[0]], refs[sizes[0] : sum(sizes)]]
+    (m_ref, band_ref, own_ref, out_ref, flat, pr, pi, mr, mi, m_half, wide, cov_b, cov_a, y_ref, low_ref, diag) = refs[
+        sum(sizes) :
+    ]
+    step = pl.program_id(0)
+    half = groups[0][-1].shape[1]
     dates = 2 * half
-    wins = lines // 4 - 3
-    load_planes([z_ref, z2_ref], m_ref, flat, pr, pi, mr, mi, m_half)
-    window_sums(dates, step % 2 == 1, band_ref, pr, pi, mr, mi, wide, cov_a, cov_b)
+    wins = m_ref.shape[0] // 4 - 3
+    load_planes(width, groups, m_ref, flat, pr, pi, mr, mi, m_half)
+    all_sums(dates, band_ref, pr, pi, mr, mi, wide, cov_a, cov_b)
 
     @pl.when((step % 2 == 0) & (step > 0))
     def _():
@@ -301,7 +321,10 @@
 
 
 def call_windows(groups, mask, win_cols, own=None):
-    count, lines = groups[0].shape[1:3]
+    count = groups[0][-1].shape[1]
+    lines = mask.shape[0]
+    width = groups[0][0].shape[3]
+    sizes = [len(group) for group in groups]
     dates = count * len(groups)
     wins = lines // 4 - 3
     steps = 2 * (win_cols // LANES) + 1
@@ -319,10 +342,11 @@
     f32 = jnp.float32
     place = lambda t: jnp.maximum((t + 1) // 2 - 1, 0)
     cov_spec = pl.BlockSpec((count, wins, 2, count, LANES), lambda t: (0, 0, 0, 0, place(t)))
-    in_specs = [pl.BlockSpec((2, count, lines, STEP), lambda t: (0, 0, 0, t)) for _ in groups]
+    operands = [array for group in groups for array in group]
+    in_specs = [pl.BlockSpec(array.shape[:3] + (STEP,), lambda t: (0, 0, 0, t)) for array in operands]
     in_specs.append(pl.BlockSpec((lines, STEP), lambda t: (0, t)))
     in_specs.append(pl.BlockSpec((1, STEP, 2 * LANES), lambda t: (t % 2, 0, 0)))
-    operands = list(groups) + [mask, bands]
+    operands += [mask, bands]
     scratch = [
         pltpu.VMEM((2, 2 * dates * pitch, LANES), f32),
         pltpu.VMEM((2, lines, count, LANES), f32),
@@ -350,7 +374,7 @@
             pltpu.VMEM((dates, LANES), f32),
         ]
     return pl.pallas_call(
-        kernel,
+        functools.partial(kernel, width, sizes),
         grid=(steps,),
         in_specs=in_specs,
         out_specs=out_spec,
@@ -374,22 +398,22 @@
         wide = jnp.pad(array, ((0, 0),) * (array.ndim - 1) + ((HALO, HALO),))
         return lax.dynamic_slice_in_dim(wide, number * tile, width, array.ndim - 1)
 
-    def edges(array):
-        dim = array.ndim - 2
+    def edges(arrays):
         count = lax.axis_size("az")
-        head = lax.slice_in_dim(array, 0, HALO, axis=dim)
-        tail = lax.slice_in_dim(array, lines - HALO, lines, axis=dim)
-        before = lax.ppermute(tail, "az", [(i, i + 1) for i in range(count - 1)])
-        after = lax.ppermute(head, "az", [(i + 1, i) for i in range(count - 1)])
-        return jnp.concatenate([before, array, after], axis=dim)
-
-    def spare(array):
-        return jnp.pad(array, ((0, 0),) * (array.ndim - 1) + ((0, padded_width - width),))
-
-    mask = spare(edges(cut(scatter_mask, own).astype(jnp.bfloat16))).astype(jnp.float32)
+        dim = arrays[0].ndim - 2
+        join = lambda start: jnp.concatenate([lax.slice_in_dim(a, start, start + HALO, axis=dim) for a in arrays], axis=dim - 1)
+        before = lax.ppermute(join(lines - HALO), "az", [(i, i + 1) for i in range(count - 1)])
+        after = lax.ppermute(join(0), "az", [(i + 1, i) for i in range(count - 1)])
+        return [before, after]
+
+    mask = cut(scatter_mask, own).astype(jnp.bfloat16)
+    above, below = edges([mask[None]])
+    mask = jnp.concatenate([above[0], mask, below[0]], axis=0)
+    mask = jnp.pad(mask, ((0, 0), (0, padded_width - width))).astype(jnp.float32)
+    first = max(1, dates_here // 4)
     pieces = [[] for _ in range(parts)]
-    for chunk in range(CHUNKS):
-        filtered = filter_lines(stack, range_filter, chunk, CHUNKS)
+    for skip, here in ((0, first), (first, dates_here - first)):
+        filtered = filter_lines(stack, range_filter, skip, here)
         sent = [cut(filtered, lax.rem(own + shift, parts)) for shift in range(1, parts)]
         stack, sent = lax.optimization_barrier((stack, sent))
         pieces[0].append(cut(filtered, own))
@@ -397,11 +421,11 @@
             pieces[shift].append(lax.ppermute(sent[shift - 1], "dr", [(i, (i + shift) % parts) for i in range(parts)]))
     near = sum(pieces[: parts // 2], [])
     far = sum(pieces[parts // 2 :], [])
-    near = spare(edges(jnp.concatenate(near, axis=1)))
+    near, far[0] = lax.optimization_barrier((near, far[0]))
+    near = near + edges(near)
     own_sums = call_windows([near], mask, win_cols)
     own_sums, far = lax.optimization_barrier((own_sums, far))
-    far = spare(edges(jnp.concatenate(far, axis=1)))
-    linked = call_windows([near, far], mask, win_cols, own_sums)
+    linked = call_windows([near, far + edges(far)], mask, win_cols, own_sums)
     wins = linked.shape[0]
     linked = jnp.transpose(linked, (1, 2, 0, 3)).reshape(2, parts, dates_here, wins, win_cols)
     ordered = [

time: 291 us -> 267 us (0.918)
  other arithmetic: 13.7 us -> 3.1 us
  waiting for transfers between devices: 33.8 us -> 27.4 us
  Pallas kernels: 201 us -> 197 us
    concatenate x2 -> x4, other arithmetic: 11.6 us -> 1.12 us  [edges(): jnp.concatenate([lax.slice_in_dim(a, start, start + HALO, axis=dim) for a...]
    ppermute x2, waiting for transfers between devices: 6.48 us -> 0.01 us  [on_device(): lax.ppermute(sent[shift - 1], 'dr', [(i, (i + shift) % parts) for i in ra...]
    pallas_call x2, Pallas kernels: 153 us -> 150 us  [call_windows(): pl.pallas_call(functools.partial(kernel, width, sizes), grid=(steps,), in...]
    unnamed x13 -> x20, local copies, waits for them, and re-layouts: 8.01 us -> 5.34 us
  transfers between devices with their start and end apart: 8 -> 8, of which waited for: 4 -> 2; matrix products, arithmetic and copies ran while one was open for 3% -> 4% of each run, Pallas kernels for 15% -> 29%
where the time goes in v3:
time: 267 us
  Pallas kernels  197 us (74%)
  waiting for transfers between devices  27.4 us (10%)
  starting transfers between devices  20.3 us (8%)
  local copies, waits for them, and re-layouts  19.3 us (7%)
  other arithmetic  3.1 us (1%)
    pallas_call x2, Pallas kernels, call_windows(): pl.pallas_call(functools.partial(kernel, width, sizes), grid=(steps,), in...  150 us
    pallas_call x2, Pallas kernels, filter_lines(): pl.pallas_call(functools.partial(filter_kernel, outer), grid=(here,), in_...  47.2 us
    ppermute x3, waiting for transfers between devices, edges(): lax.ppermute(join(lines - HALO), 'az', [(i, i + 1) for i in range(count -...  27.4 us
    ppermute x3, starting transfers between devices, edges(): lax.ppermute(join(lines - HALO), 'az', [(i, i + 1) for i in range(count -...  12.2 us
    ppermute x3, starting transfers between devices, edges(): after = lax.ppermute(join(0), 'az', [(i + 1, i) for i in range(count - 1)])  5.94 us
  transfers between devices with their start and end apart: 8, of which 2 were waited for; matrix products, arithmetic and copies ran while one was open for 4% of the time, Pallas kernels for 29%

profile of v3, /device:TPU:1, one launch (start us, length us, event | category | flops | bytes accessed | tf_op | source)
XLA Modules:
  0.0 267.1 jit_solution(8287144215378113644)
XLA Ops:
  0.0 0.0 copy-start.1
  0.0 0.0 copy-start.2
  0.0 0.0 copy-start.3
  0.0 1.3 reshape.7
  1.4 0.3 copy.17
  1.7 0.0 copy-done.1
  1.7 0.0 copy-done.2
  1.7 0.0 copy-done.3
  1.7 0.0 copy-start
  1.7 2.8 %copy-done = bf16[2,16,24,4096]{3,2,1,0:T(8,128)(2,1)S(1)} copy-done((bf16[2,16,24,4096]{3,2,1,0:T(8,128)(2,1)S(1)}, bf16[2,16,24,4096]{3,2,1,0:T(8,128)(2,1)}, u32[]{:S(2)}) %copy-start) | copy-done | bytes 6291480
  4.5 11.8 %shard_map.109 = bf16[2,4,24,4096]{3,2,1,0:T(8,128)(2,1)S(1)} custom-call(bf16[2,16,24,4096]{3,2,1,0:T(8,128)(2,1)S(1)} %copy-done, f32[16,32,128]{2,1,0:T(8,128)S(1)} %bitcast.12, f32[32,128]{1,0:T(8,128)S(1)} %copy-done.3, f32[32,128]{1,0:T(8,128)S(1)} %copy-done.2, bf16[4,256,256]{2,1,0:T(8,128)(2,1)S(1)} %copy-done.1), custom_call_target="tpu_custom_call" | custom-call | flops 400000000 | bytes 1000000 | tf_op jit(solution)/shard_map/pallas_call | solution.py:128
  16.3 1.0 pad_dynamic-slice_fusion.2
  17.2 0.0 copy-start.5
  17.3 2.1 collective-permute-start
  19.4 35.4 %shard_map.110 = bf16[2,12,24,4096]{3,2,1,0:T(8,128)(2,1)S(1)} custom-call(bf16[2,16,24,4096]{3,2,1,0:T(8,128)(2,1)S(1)} %copy-done, f32[16,32,128]{2,1,0:T(8,128)S(1)} %bitcast.13, f32[32,128]{1,0:T(8,128)S(1)} %copy-done.3, f32[32,128]{1,0:T(8,128)S(1)} %copy-done.2, bf16[4,256,256]{2,1,0:T(8,128)(2,1)S(1)} %copy-done.1), custom_call_target="tpu_custom_call" | custom-call | flops 1200000000 | bytes 1000000 | tf_op jit(solution)/shard_map/pallas_call | solution.py:128
  54.8 0.0 copy-start.9
  54.8 4.4 %pad_dynamic-slice_fusion = (bf16[2,12,24,2060]{3,2,1,0:T(8,128)(2,1)}, bf16[2,12,24,2060]{3,2,1,0:T(8,128)(2,1)S(1)}) fusion(s32[]{:T(128)S(6)} %select_n.17, bf16[2,12,24,4096]{3,2,1,0:T(8,128)(2,1)S(1)} %shard_map.110, s32[]{:T(128)S(6)} %select_n.16), kind=kLoop, calls=%fused_computation | loop fusion | bytes 9464840 | tf_op jit(solution)/shard_map/dynamic_slice | solution.py:399
  59.2 0.0 collective-permute-start.5
  59.2 0.0 copy-done.9
  59.2 0.1 fusion.12
  59.3 0.0 collective-permute-done.refs_4_
  59.3 0.0 copy-start.7
  59.3 1.0 copy-done.7
  60.4 0.2 fusion.8
  60.6 0.0 copy-done.5
  60.6 0.3 copy-done.4
  60.9 0.1 fusion.10
  61.0 0.3 pad_maximum_fusion.1
  61.3 0.1 copy.19
  61.4 0.3 pad_maximum_fusion
  61.7 0.1 copy.18
  61.8 4.2 %collective-permute-start.1 = (bf16[2,16,6,2060]{3,1,2,0:T(8,128)(2,1)S(1)}, bf16[2,16,6,2060]{3,1,2,0:T(8,128)(2,1)S(1)}, u32[]{:S(2)}, u32[]{:S(2)}) collective-permute-start(bf16[2,16,6,2060]{3,1,2,0:T(8,128)(2,1)S(1)} %copy.18), channel_id=1, source_target_pairs={{0,2},{2,4},{4,6},{6,8},{8,10},{10,12},{12,14},{14,16},{16,18},{18... | collective-permute-start | bytes 2373128 | tf_op jit(solution)/shard_map/ppermute | solution.py:405
  65.9 1.9 collective-permute-start.2
  67.9 3.6 %collective-permute-start.3 = (bf16[1,6,2060]{2,1,0:T(8,128)(2,1)S(1)}, bf16[1,6,2060]{2,1,0:T(8,128)(2,1)S(1)}, u32[]{:S(2)}, u32[]{:S(2)}) collective-permute-start(bf16[1,6,2060]{2,1,0:T(8,128)(2,1)S(1)} %get-tuple-element.37), channel_id=1, source_target_pairs={{0,2},{2,4},{4,6},{6,8},{8,10},{10,12},{12,14},{14,16},{16,18},{18... | collective-permute-start | bytes 74168 | tf_op jit(solution)/shard_map/ppermute | solution.py:405
  71.5 1.9 collective-permute-start.4
  73.5 0.1 fusion.3
  73.6 11.5 %collective-permute-done.3 = bf16[1,6,2060]{2,1,0:T(8,128)(2,1)S(1)} collective-permute-done((bf16[1,6,2060]{2,1,0:T(8,128)(2,1)S(1)}, bf16[1,6,2060]{2,1,0:T(8,128)(2,1)S(1)}, u32[]{:S(2)}, u32[]{:S(2)}) %collective-permute-start.3) | collective-permute-done | bytes 24752 | tf_op jit(solution)/shard_map/ppermute | solution.py:405
  85.1 0.0 collective-permute-done.4
  85.1 0.8 fusion.6.refs_4_.refs_8_
  85.9 0.0 collective-permute-done.1
  85.9 1.2 copy.24.refs_2_
  87.1 0.0 collective-permute-done.2
  87.1 1.2 copy.25.refs_3_
  88.3 43.3 %shard_map.111.refs_10_ = f32[16,6,2,16,512]{4,3,2,1,0:T(8,128)} custom-call(bf16[2,4,24,2060]{3,2,1,0:T(8,128)(2,1)} %copy-done.5, bf16[2,12,24,2060]{3,2,1,0:T(8,128)(2,1)} %copy-done.4, bf16[2,16,6,2060]{3,2,1,0:T(8,128)(2,1)} %copy.24.refs_2_, bf16[2,16,6,2060]{3,2,1,0:T(8,128)(2,1)} %copy.25.refs_3_, f32[36,2304]{1,0:T(8,128)} %fusion.6.refs_4_.refs_8_, ...), custom_call_target="tpu_custom_call" | custom-call | flops 900000000 | bytes 1000000 | tf_op jit(solution)/shard_map/pallas_call | solution.py:376
  131.7 0.0 collective-permute-done.5.refs_5_
  131.7 0.0 copy-done.8
  131.7 0.0 copy-start.6
  131.7 0.1 fusion.9
  131.7 0.2 fusion.7
  132.0 1.1 copy-done.6
  133.1 0.3 pad_maximum_fusion.2
  133.4 0.1 copy.22
  133.5 4.4 %collective-permute-start.6 = (bf16[2,16,6,2060]{3,1,2,0:T(8,128)(2,1)S(1)}, bf16[2,16,6,2060]{3,1,2,0:T(8,128)(2,1)S(1)}, u32[]{:S(2)}, u32[]{:S(2)}) collective-permute-start(bf16[2,16,6,2060]{3,1,2,0:T(8,128)(2,1)S(1)} %copy.22), channel_id=1, source_target_pairs={{0,2},{2,4},{4,6},{6,8},{8,10},{10,12},{12,14},{14,16},{16,18},{18... | collective-permute-start | bytes 2373128 | tf_op jit(solution)/shard_map/ppermute | solution.py:405
  137.9 0.3 pad_maximum_fusion.3
  138.2 0.1 copy.23
  138.3 2.1 collective-permute-start.7
  140.4 15.9 %collective-permute-done.6 = bf16[2,16,6,2060]{3,1,2,0:T(8,128)(2,1)S(1)} collective-permute-done((bf16[2,16,6,2060]{3,1,2,0:T(8,128)(2,1)S(1)}, bf16[2,16,6,2060]{3,1,2,0:T(8,128)(2,1)S(1)}, u32[]{:S(2)}, u32[]{:S(2)}) %collective-permute-start.6) | collective-permute-done | bytes 791072 | tf_op jit(solution)/shard_map/ppermute | solution.py:405
  156.3 1.2 copy.26.refs_6_
  157.5 0.0 collective-permute-done.7
  157.5 1.2 copy.27.refs_7_
  158.7 106.2 %shard_map.112 = f32[6,2,32,512]{3,2,1,0:T(8,128)} custom-call(bf16[2,4,24,2060]{3,2,1,0:T(8,128)(2,1)} %copy-done.5, bf16[2,12,24,2060]{3,2,1,0:T(8,128)(2,1)} %copy-done.4, bf16[2,16,6,2060]{3,2,1,0:T(8,128)(2,1)} %copy.24.refs_2_, bf16[2,16,6,2060]{3,2,1,0:T(8,128)(2,1)} %copy.25.refs_3_, bf16[2,4,24,2060]{3,2,1,0:T(8,128)(2,1)} %copy-done.7, ...), custom_call_target="tpu_custom_call" | custom-call | flops 900000000 | bytes 1000000 | tf_op jit(solution)/shard_map/pallas_call | solution.py:376
  264.9 1.2 constant_dynamic-slice_fusion
  266.1 0.1 copy_bitcast_fusion
  266.1 0.9 pad_maximum_fusion.4
  (3 shorter events, 0.0 us)
Async XLA Ops:
  0.0 1.7 copy-start.1
  0.0 1.7 copy-start.2
  0.0 1.7 copy-start.3
  1.7 2.8 %copy-start = (bf16[2,16,24,4096]{3,2,1,0:T(8,128)(2,1)S(1)}, bf16[2,16,24,4096]{3,2,1,0:T(8,128)(2,1)}, u32[]{:S(2)}) copy-start(bf16[2,16,24,4096]{3,2,1,0:T(8,128)(2,1)} %x_ref.2) | copy-start | bytes 18874372
  17.2 43.3 %copy-start.5 = (bf16[2,4,24,2060]{3,2,1,0:T(8,128)(2,1)}, bf16[2,4,24,2060]{3,2,1,0:T(8,128)(2,1)S(1)}, u32[]{:S(2)}) copy-start(bf16[2,4,24,2060]{3,2,1,0:T(8,128)(2,1)S(1)} %get-tuple-element.16.refs_0_) | copy-start | bytes 2373124
  17.3 42.1 %collective-permute-start = (bf16[2,4,24,2060]{3,2,1,0:T(8,128)(2,1)S(1)}, bf16[2,4,24,2060]{3,2,1,0:T(8,128)(2,1)S(1)}, u32[]{:S(2)}, u32[]{:S(2)}) collective-permute-start(bf16[2,4,24,2060]{3,2,1,0:T(8,128)(2,1)S(1)} %get-tuple-element.15), channel_id=1, source_target_pairs={{0,1},{1,0},{2,3},{3,2},{4,5},{5,4},{6,7},{7,6},{8,9},{9,8},{10,11... | collective-permute-start | bytes 2373128 | tf_op jit(solution)/shard_map/ppermute | solution.py:421
  54.8 4.4 %copy-start.9 = (s32[24,4096]{1,0:T(8,128)S(1)}, s32[24,4096]{1,0:T(8,128)}, u32[]{:S(2)}) copy-start(s32[24,4096]{1,0:T(8,128)} %param.13) | copy-start | bytes 1179652
  59.2 1.8 copy-start.4
  59.2 72.5 %collective-permute-start.5 = (bf16[2,12,24,2060]{3,2,1,0:T(8,128)(2,1)}, bf16[2,12,24,2060]{3,2,1,0:T(8,128)(2,1)S(1)}, u32[]{:S(2)}, u32[]{:S(2)}) collective-permute-start(bf16[2,12,24,2060]{3,2,1,0:T(8,128)(2,1)} %get-tuple-element.19), channel_id=1, source_target_pairs={{0,1},{1,0},{2,3},{3,2},{4,5},{5,4},{6,7},{7,6},{8,9},{9,8},{10,11... | collective-permute-start | bytes 7119368 | tf_op jit(solution)/shard_map/ppermute | solution.py:421
  59.3 1.1 copy-start.7
  61.8 24.1 %collective-permute-start.1 = (bf16[2,16,6,2060]{3,1,2,0:T(8,128)(2,1)S(1)}, bf16[2,16,6,2060]{3,1,2,0:T(8,128)(2,1)S(1)}, u32[]{:S(2)}, u32[]{:S(2)}) collective-permute-start(bf16[2,16,6,2060]{3,1,2,0:T(8,128)(2,1)S(1)} %copy.18), channel_id=1, source_target_pairs={{0,2},{2,4},{4,6},{6,8},{8,10},{10,12},{12,14},{14,16},{16,18},{18... | collective-permute-start | bytes 2373128 | tf_op jit(solution)/shard_map/ppermute | solution.py:405
  65.9 21.2 %collective-permute-start.2 = (bf16[2,16,6,2060]{3,1,2,0:T(8,128)(2,1)S(1)}, bf16[2,16,6,2060]{3,1,2,0:T(8,128)(2,1)S(1)}, u32[]{:S(2)}, u32[]{:S(2)}) collective-permute-start(bf16[2,16,6,2060]{3,1,2,0:T(8,128)(2,1)S(1)} %copy.19), channel_id=1, source_target_pairs={{2,0},{4,2},{6,4},{8,6},{10,8},{12,10},{14,12},{16,14},{18,16},{20... | collective-permute-start | bytes 2373128 | tf_op jit(solution)/shard_map/ppermute | solution.py:406
  67.9 17.2 %collective-permute-start.3 = (bf16[1,6,2060]{2,1,0:T(8,128)(2,1)S(1)}, bf16[1,6,2060]{2,1,0:T(8,128)(2,1)S(1)}, u32[]{:S(2)}, u32[]{:S(2)}) collective-permute-start(bf16[1,6,2060]{2,1,0:T(8,128)(2,1)S(1)} %get-tuple-element.37), channel_id=1, source_target_pairs={{0,2},{2,4},{4,6},{6,8},{8,10},{10,12},{12,14},{14,16},{16,18},{18... | collective-permute-start | bytes 74168 | tf_op jit(solution)/shard_map/ppermute | solution.py:405
  71.5 13.5 %collective-permute-start.4 = (bf16[1,6,2060]{2,1,0:T(8,128)(2,1)S(1)}, bf16[1,6,2060]{2,1,0:T(8,128)(2,1)S(1)}, u32[]{:S(2)}, u32[]{:S(2)}) collective-permute-start(bf16[1,6,2060]{2,1,0:T(8,128)(2,1)S(1)} %get-tuple-element.38), channel_id=1, source_target_pairs={{2,0},{4,2},{6,4},{8,6},{10,8},{12,10},{14,12},{16,14},{18,16},{20... | collective-permute-start | bytes 74168 | tf_op jit(solution)/shard_map/ppermute | solution.py:406
  88.3 43.3 %copy-start.8 = (bf16[2,4,24,2060]{3,2,1,0:T(8,128)(2,1)S(1)}, bf16[2,4,24,2060]{3,2,1,0:T(8,128)(2,1)}, u32[]{:S(2)}) copy-start(bf16[2,4,24,2060]{3,2,1,0:T(8,128)(2,1)} %copy-done.7) | copy-start | bytes 2373124
  131.7 1.4 copy-start.6
  133.5 22.8 %collective-permute-start.6 = (bf16[2,16,6,2060]{3,1,2,0:T(8,128)(2,1)S(1)}, bf16[2,16,6,2060]{3,1,2,0:T(8,128)(2,1)S(1)}, u32[]{:S(2)}, u32[]{:S(2)}) collective-permute-start(bf16[2,16,6,2060]{3,1,2,0:T(8,128)(2,1)S(1)} %copy.22), channel_id=1, source_target_pairs={{0,2},{2,4},{4,6},{6,8},{8,10},{10,12},{12,14},{14,16},{16,18},{18... | collective-permute-start | bytes 2373128 | tf_op jit(solution)/shard_map/ppermute | solution.py:405
  138.3 19.2 %collective-permute-start.7 = (bf16[2,16,6,2060]{3,1,2,0:T(8,128)(2,1)S(1)}, bf16[2,16,6,2060]{3,1,2,0:T(8,128)(2,1)S(1)}, u32[]{:S(2)}, u32[]{:S(2)}) collective-permute-start(bf16[2,16,6,2060]{3,1,2,0:T(8,128)(2,1)S(1)} %copy.23), channel_id=1, source_target_pairs={{2,0},{4,2},{6,4},{8,6},{10,8},{12,10},{14,12},{16,14},{18,16},{20... | collective-permute-start | bytes 2373128 | tf_op jit(solution)/shard_map/ppermute | solution.py:406
